TPU v7x, 512 devices: a whole 4x8x8 slice. The times are simulated.
512 devices in a mesh: tile: 128 (over y, z, core), col: 4 (over x).
Axes of the slice: x: 4, y: 8, z: 8, core: 2. Of those that a mesh axis runs over, the one named last changes fastest.
Arguments:
- block: float32 [128, 294912], P('col', 'tile'), may hold values from -6 to 6
- tiles: float32 [3072, 4, 9216], P('tile'), may hold values from -0.625 to 0.625
- intact: int32 [3072, 4, 96], P('tile'), may hold values 0 or 1
- adjacency: int32 [3072, 4], P('tile'), may hold values from 1 to 3
- stiff_diag: float32 [294912], P('tile'), may hold values from 4 to 40
- cut_low: float32 [1], replicated, may hold values from 14 to 18
- cut_high: float32 [1], replicated, may hold values from 42 to 48
Outputs:
- basis: float32 [128, 294912], P('col', 'tile')
- reduced: float32 [128, 128], replicated
All inputs are finite; a program needn't handle non-finite values. No bound on the sum of `intact` on one device may be relied on, other than what follows from the above.
Results may differ from a plain program's by a relative error of at most 0.00017.
Values sent between devices are 32-bit elements; how exact they have to be, the bound alone decides.
A program may use at most 64 MiB of HBM per device.

v0:
```python
import jax
import jax.numpy as jnp
from jax import lax
from jax.sharding import PartitionSpec as P

R = 3


HIGH = lax.Precision.HIGHEST


def shifted(value, axis, steps):
    count = lax.axis_size(axis)
    initial, last = (max(0, -steps), min(count, count - steps))
    return lax.ppermute(value, axis, [(source, source + steps) for source in range(initial, last)])


def inner(left, right):
    return lax.dot_general(
        left, right, (((1,), (1,)), ((), ())), precision=HIGH, preferred_element_type=jnp.float32
    )


def local(block, tiles, intact, adjacency, stiff_diag, cut_low, cut_high):
    cols = block.shape[0]
    nblk = tiles.shape[0]
    slots = tiles.shape[1]
    width = intact.shape[2]
    reach = R
    coupling = intact.astype(jnp.float32)[..., None] * tiles.reshape(nblk, slots, width, width)
    local_index = jnp.arange(nblk, dtype=jnp.int32)
    target = local_index[:, None] + adjacency

    def apply_stiffness(rows):
        blocks = rows.reshape(cols, nblk, width)
        ahead = shifted(blocks[:, :reach], "tile", -1)
        extended = jnp.concatenate([blocks, ahead], 1)
        back = jnp.einsum("jsab,mja->mjsb", coupling, blocks, precision=HIGH)
        landing = (
            target[..., None] == jnp.arange(nblk + reach, dtype=jnp.int32)[None, None, :]
        ).astype(jnp.float32)
        spread_all = jnp.einsum("mjsb,jsq->mqb", back, landing, precision=HIGH)
        spilled = shifted(spread_all[:, nblk:], "tile", 1)
        spread = spread_all[:, :nblk] + jnp.pad(spilled, ((0, 0), (0, nblk - reach), (0, 0)))
        neighbours = jnp.take(extended, target, axis=1)
        front = jnp.einsum("jsab,mjsb->mja", coupling, neighbours, precision=HIGH)
        return stiff_diag[None, :] * rows - (front + spread).reshape(rows.shape)

    center = (cut_low[0] + cut_high[0]) / 2.0
    half = (cut_high[0] - cut_low[0]) / 2.0
    first = (apply_stiffness(block) - center * block) / half
    filtered = 2.0 * (apply_stiffness(first) - center * first) / half - block
    stiff = apply_stiffness(filtered)
    total = nblk * width * lax.axis_size("tile")
    whole_rows, whole_stiff = (
        lax.all_gather(filtered, "col", axis=0, tiled=True),
        lax.all_gather(stiff, "col", axis=0, tiled=True),
    )
    gram, proj = lax.psum(
        (inner(whole_rows, whole_rows) / total, inner(whole_stiff, whole_rows) / total), "tile"
    )
    full = gram.shape[0]
    lower = jnp.linalg.cholesky(gram)
    inverse = jax.scipy.linalg.solve_triangular(lower, jnp.eye(full, dtype=jnp.float32), lower=True)
    start = lax.axis_index("col") * cols
    my_inverse = lax.dynamic_slice_in_dim(inverse, start, cols, 0)
    basis = jnp.dot(my_inverse, whole_rows, precision=HIGH, preferred_element_type=jnp.float32)
    reduced = (
        jnp.dot(jnp.dot(inverse, proj, precision=HIGH), inverse.T, precision=HIGH) / cut_high[0]
    )
    return (basis, reduced)


def solution(mesh):
    in_specs = (
        P("col", "tile"),
        P("tile", None, None),
        P("tile", None, None),
        P("tile", None),
        P("tile"),
        P(),
        P(),
    )
    out_specs = (P("col", "tile"), P())
    return jax.shard_map(local, mesh=mesh, in_specs=in_specs, out_specs=out_specs, check_vma=False)
```

profile of v0, /device:TPU:1, one launch (start us, length us, event | category | flops | bytes accessed | tf_op | source)
XLA Modules:
  0.0 355.1 jit_solution(2789210036545248543)
XLA Ops:
  7.2 5.9 %reshape.44 = f32[24,4,96,96]{3,2,1,0:T(8,128)} reshape(f32[24,4,9216]{2,1,0:T(4,128)} %param.10) | data formatting | bytes 7077888 | tf_op jit(solution)/shard_map/reshape | solution.py:30
  13.5 5.1 %fusion.30 = f32[32,24,4,96]{3,0,2,1:T(8,128)S(1)} fusion(f32[24,4,96,96]{3,2,1,0:T(8,128)} %reshape.44, f32[24,4,96]{2,1,0:T(4,128)S(1)} %convert_element_type.6, f32[32,24,96,1]{2,1,0,3:T(8,128)S(1)} %bitcast.106), kind=kOutput, calls=%fused_computation.33 | convolution fusion | flops 340623360 | bytes 5050368 | tf_op jit(solution)/shard_map/jsab,mja->mjsb/dot_general | solution.py:38
  18.5 1.6 fusion.39
  20.4 5.4 %collective-permute-start.1 = (f32[32,3,96]{2,0,1:T(8,128)S(1)}, f32[32,3,96]{2,0,1:T(8,128)S(1)}, u32[]{:S(2)}, u32[]{:S(2)}) collective-permute-start(f32[32,3,96]{2,0,1:T(8,128)S(1)} %slice.56), channel_id=1, source_target_pairs={{0,4},{4,8},{8,12},{12,16},{16,20},{20,24},{24,28},{28,32},{32,36}... | collective-permute-start | bytes 110600 | tf_op jit(solution)/shard_map/ppermute | solution.py:15
  25.9 4.7 %collective-permute-start = (f32[32,3,96]{2,0,1:T(8,128)S(1)}, f32[32,3,96]{2,0,1:T(8,128)S(1)}, u32[]{:S(2)}, u32[]{:S(2)}) collective-permute-start(f32[32,3,96]{2,0,1:T(8,128)S(1)} %slice.54), channel_id=1, source_target_pairs={{4,0},{8,4},{12,8},{16,12},{20,16},{24,20},{28,24},{32,28},{36,32}... | collective-permute-start | bytes 110600 | tf_op jit(solution)/shard_map/ppermute | solution.py:15
  33.0 6.5 %fusion.73 = f32[32,24,96]{2,0,1:T(8,128)S(1)} fusion(f32[24,4,96,96]{3,2,1,0:T(8,128)} %reshape.44, f32[24,4,96]{2,1,0:T(4,128)S(1)} %convert_element_type.6, f32[24,4,32,96]{3,2,1,0:T(8,128)S(1)} %bitcast.103, pred[24,4]{1,0:T(8,128)(4,1)S(1)} %copy.37, f32[32,27,96]{2,0,1:T(8,128)S(1)} %bitcast.109, f32[32,3,96]{2,0,1:T(8,128)S(1)} %collective-permute-done.1), kind=kOutput, calls=%fused_computation.44 | convolution fusion | flops 341065728 | bytes 5382240 | tf_op jit(solution)/shard_map/jsab,mjsb->mja/dot_general | solution.py:46
  40.4 1.9 collective-permute-start.2
  42.3 5.1 %fusion.33 = f32[32,24,4,96]{3,0,2,1:T(8,128)S(1)} fusion(f32[24,4,96,96]{3,2,1,0:T(8,128)} %reshape.44, f32[24,4,96]{2,1,0:T(4,128)S(1)} %convert_element_type.6, f32[32,24,96,1]{2,1,0,3:T(8,128)S(1)} %bitcast.107), kind=kOutput, calls=%fused_computation.34 | convolution fusion | flops 340623360 | bytes 5050368 | tf_op jit(solution)/shard_map/jsab,mja->mjsb/dot_general | solution.py:38
  47.4 1.6 fusion.42
  49.3 3.8 %collective-permute-start.3 = (f32[32,3,96]{2,0,1:T(8,128)S(1)}, f32[32,3,96]{2,0,1:T(8,128)S(1)}, u32[]{:S(2)}, u32[]{:S(2)}) collective-permute-start(f32[32,3,96]{2,0,1:T(8,128)S(1)} %slice.59), channel_id=1, source_target_pairs={{0,4},{4,8},{8,12},{12,16},{16,20},{20,24},{24,28},{28,32},{32,36}... | collective-permute-start | bytes 110600 | tf_op jit(solution)/shard_map/ppermute | solution.py:15
  54.1 6.5 %fusion.68 = f32[32,24,96]{2,0,1:T(8,128)S(1)} fusion(f32[24,4,96,96]{3,2,1,0:T(8,128)} %reshape.44, f32[24,4,96]{2,1,0:T(4,128)S(1)} %convert_element_type.6, f32[24,4,32,96]{3,2,1,0:T(8,128)S(1)} %bitcast.104, pred[24,4]{1,0:T(8,128)(4,1)S(1)} %copy.37, f32[32,27,96]{2,0,1:T(8,128)S(1)} %bitcast.113, f32[32,3,96]{2,0,1:T(8,128)S(1)} %collective-permute-done.3), kind=kOutput, calls=%fused_computation.43 | convolution fusion | flops 341065728 | bytes 5382240 | tf_op jit(solution)/shard_map/jsab,mjsb->mja/dot_general | solution.py:46
  62.0 1.9 collective-permute-start.4
  63.9 5.1 %fusion.36 = f32[32,24,4,96]{3,0,2,1:T(8,128)S(1)} fusion(f32[24,4,96,96]{3,2,1,0:T(8,128)} %reshape.44, f32[24,4,96]{2,1,0:T(4,128)S(1)} %convert_element_type.6, f32[32,24,96,1]{2,1,0,3:T(8,128)S(1)} %bitcast.105), kind=kOutput, calls=%fused_computation.35 | convolution fusion | flops 340623360 | bytes 5050368 | tf_op jit(solution)/shard_map/jsab,mja->mjsb/dot_general | solution.py:38
  69.0 1.6 fusion.45
  70.9 4.2 %collective-permute-start.5 = (f32[32,3,96]{2,0,1:T(8,128)S(1)}, f32[32,3,96]{2,0,1:T(8,128)S(1)}, u32[]{:S(2)}, u32[]{:S(2)}) collective-permute-start(f32[32,3,96]{2,0,1:T(8,128)S(1)} %slice.62), channel_id=1, source_target_pairs={{0,4},{4,8},{8,12},{12,16},{16,20},{20,24},{24,28},{28,32},{32,36}... | collective-permute-start | bytes 110600 | tf_op jit(solution)/shard_map/ppermute | solution.py:15
  76.3 6.5 %fusion.63 = f32[32,24,96]{2,0,1:T(8,128)S(1)} fusion(f32[24,4,96,96]{3,2,1,0:T(8,128)} %reshape.44, f32[24,4,96]{2,1,0:T(4,128)S(1)} %convert_element_type.6, f32[24,4,32,96]{3,2,1,0:T(8,128)S(1)} %bitcast.102, pred[24,4]{1,0:T(8,128)(4,1)S(1)} %copy.37, f32[32,27,96]{2,0,1:T(8,128)S(1)} %bitcast.111, f32[32,3,96]{2,0,1:T(8,128)S(1)} %collective-permute-done.5), kind=kOutput, calls=%fused_computation.42 | convolution fusion | flops 341065728 | bytes 5382240 | tf_op jit(solution)/shard_map/jsab,mjsb->mja/dot_general | solution.py:46
  84.8 14.2 %all-gather.3.cloned.1.call-done = f32[128,2304]{1,0:T(8,128)} async-done(((f32[32,2304]{1,0:T(8,128)}), f32[128,2304]{1,0:T(8,128)}) %all-gather.3.cloned.1.call-update) | async-done | bytes 1179664 | tf_op jit(solution)/shard_map/all_gather | solution.py:56
  99.0 3.5 convolution_multiply_fusion.1
  102.4 29.0 %all-gather.5.cloned.1.call-done = f32[128,2304]{1,0:T(8,128)} async-done(((f32[32,2304]{1,0:T(8,128)}), f32[128,2304]{1,0:T(8,128)}) %all-gather.5.cloned.1.call-update) | async-done | bytes 1179664 | tf_op jit(solution)/shard_map/all_gather | solution.py:57
  131.4 3.0 convolution_multiply_fusion
  134.5 185.7 %all-reduce.6.cloned.1.call-done = (f32[128,128]{0,1:T(8,128)}, f32[128,128]{0,1:T(8,128)}) async-done(((f32[128,128]{0,1:T(8,128)}, f32[128,128]{0,1:T(8,128)}), (f32[128,128]{0,1:T(8,128)}, f32[128,128]{0,1:T(8,128)})) %all-reduce.6.cloned.1.call-update) | async-done | bytes 131088 | tf_op jit(solution)/shard_map/psum | solution.py:59
  322.0 11.7 %cholesky.17 = f32[128,128]{1,0:T(8,128)S(1)} custom-call(f32[128,128]{1,0:T(8,128)S(1)} %fusion.90), custom_call_target="Cholesky" | custom-call | tf_op jit(solution)/shard_map/jit(cholesky)/cholesky | solution.py:63
  335.1 9.8 %custom-call.7 = f32[1,128,128]{1,2,0:T(8,128)S(1)} custom-call(f32[1,128,128]{2,1,0:T(8,128)S(1)} %fusion.87), custom_call_target="InvertDiagBlocksLowerTriangular" | custom-call | tf_op jit(solution)/shard_map/jit(_solve_triangular)/triangular_solve | solution.py:64
  347.1 1.4 fusion.98
  (71 shorter events, 13.9 us)
Async XLA Ops:
  7.2 6.0 %copy-start.5 = (s32[24,4,96]{2,1,0:T(4,128)S(1)}, s32[24,4,96]{2,1,0:T(4,128)}, u32[]{:S(2)}) copy-start(s32[24,4,96]{2,1,0:T(4,128)} %param.11) | copy-start | bytes 110596
  7.2 6.0 %copy-start.3 = (f32[32,2304]{1,0:T(8,128)S(1)}, f32[32,2304]{1,0:T(8,128)}, u32[]{:S(2)}) copy-start(f32[32,2304]{1,0:T(8,128)} %param.9) | copy-start | bytes 884740
  7.2 6.2 %copy-start.6 = (s32[24,4]{0,1:T(4,128)S(1)}, s32[24,4]{0,1:T(4,128)}, u32[]{:S(2)}) copy-start(s32[24,4]{0,1:T(4,128)} %param.12) | copy-start | bytes 1156
  7.2 91.8 %all-gather.3.cloned.1.call-start = ((), (), s32[]{:S(2)}) async-start(), calls=%async_computation | async-start | bytes 1474560 | tf_op jit(solution)/shard_map/all_gather | solution.py:56
  20.4 12.6 %collective-permute-start.1 = (f32[32,3,96]{2,0,1:T(8,128)S(1)}, f32[32,3,96]{2,0,1:T(8,128)S(1)}, u32[]{:S(2)}, u32[]{:S(2)}) collective-permute-start(f32[32,3,96]{2,0,1:T(8,128)S(1)} %slice.56), channel_id=1, source_target_pairs={{0,4},{4,8},{8,12},{12,16},{16,20},{20,24},{24,28},{28,32},{32,36}... | collective-permute-start | bytes 110600 | tf_op jit(solution)/shard_map/ppermute | solution.py:15
  25.9 6.3 %collective-permute-start = (f32[32,3,96]{2,0,1:T(8,128)S(1)}, f32[32,3,96]{2,0,1:T(8,128)S(1)}, u32[]{:S(2)}, u32[]{:S(2)}) collective-permute-start(f32[32,3,96]{2,0,1:T(8,128)S(1)} %slice.54), channel_id=1, source_target_pairs={{4,0},{8,4},{12,8},{16,12},{20,16},{24,20},{28,24},{32,28},{36,32}... | collective-permute-start | bytes 110600 | tf_op jit(solution)/shard_map/ppermute | solution.py:15
  33.0 6.9 %copy-start.4 = (f32[2304]{0:T(1024)S(1)}, f32[2304]{0:T(1024)}, u32[]{:S(2)}) copy-start(f32[2304]{0:T(1024)} %param.13) | copy-start | bytes 27652
  40.4 12.8 %collective-permute-start.2 = (f32[32,3,96]{2,0,1:T(8,128)S(1)}, f32[32,3,96]{2,0,1:T(8,128)S(1)}, u32[]{:S(2)}, u32[]{:S(2)}) collective-permute-start(f32[32,3,96]{2,0,1:T(8,128)S(1)} %slice.57), channel_id=1, source_target_pairs={{4,0},{8,4},{12,8},{16,12},{20,16},{24,20},{28,24},{32,28},{36,32}... | collective-permute-start | bytes 110600 | tf_op jit(solution)/shard_map/ppermute | solution.py:15
  49.3 4.8 %collective-permute-start.3 = (f32[32,3,96]{2,0,1:T(8,128)S(1)}, f32[32,3,96]{2,0,1:T(8,128)S(1)}, u32[]{:S(2)}, u32[]{:S(2)}) collective-permute-start(f32[32,3,96]{2,0,1:T(8,128)S(1)} %slice.59), channel_id=1, source_target_pairs={{0,4},{4,8},{8,12},{12,16},{16,20},{20,24},{24,28},{28,32},{32,36}... | collective-permute-start | bytes 110600 | tf_op jit(solution)/shard_map/ppermute | solution.py:15
  61.1 0.7 copy-start.1
  61.8 69.6 %all-gather.5.cloned.1.call-start = ((), (), s32[]{:S(2)}) async-start(), calls=%async_computation.1 | async-start | bytes 1474560 | tf_op jit(solution)/shard_map/all_gather | solution.py:57
  62.0 13.2 %collective-permute-start.4 = (f32[32,3,96]{2,0,1:T(8,128)S(1)}, f32[32,3,96]{2,0,1:T(8,128)S(1)}, u32[]{:S(2)}, u32[]{:S(2)}) collective-permute-start(f32[32,3,96]{2,0,1:T(8,128)S(1)} %slice.60), channel_id=1, source_target_pairs={{4,0},{8,4},{12,8},{16,12},{20,16},{24,20},{28,24},{32,28},{36,32}... | collective-permute-start | bytes 110600 | tf_op jit(solution)/shard_map/ppermute | solution.py:15
  70.9 5.4 %collective-permute-start.5 = (f32[32,3,96]{2,0,1:T(8,128)S(1)}, f32[32,3,96]{2,0,1:T(8,128)S(1)}, u32[]{:S(2)}, u32[]{:S(2)}) collective-permute-start(f32[32,3,96]{2,0,1:T(8,128)S(1)} %slice.62), channel_id=1, source_target_pairs={{0,4},{4,8},{8,12},{12,16},{16,20},{20,24},{24,28},{28,32},{32,36}... | collective-permute-start | bytes 110600 | tf_op jit(solution)/shard_map/ppermute | solution.py:15
  82.8 1.0 copy-start.2
  84.5 235.7 %all-reduce.6.cloned.1.call-start = ((), (), s32[]{:S(2)}) async-start(), calls=%async_computation.2 | async-start | bytes 262144 | tf_op jit(solution)/shard_map/psum | solution.py:59
  99.0 32.5 %copy-start = (f32[128,2304]{1,0:T(8,128)S(1)}, f32[128,2304]{1,0:T(8,128)}, u32[]{:S(2)}) copy-start(f32[128,2304]{1,0:T(8,128)} %all-gather.3.cloned.1.call-done) | copy-start | bytes 3538948
Sparse Core Ops, SparseCore 0:
  61.9 36.9 all-gather.2
  101.0 30.3 all-gather.4
  135.4 184.7 all-reduce.5
where the time goes:
time: 356 us; the launch traced here: 355 us
  waiting for transfers between devices  230 us (65%)
  matrix products  49.6 us (14%)
  other arithmetic  24.8 us (7%)
  starting transfers between devices  22.3 us (6%)
  between operations  15.5 us (4%)
  local copies, waits for them, and re-layouts  13.3 us (4%)
    psum x1, waiting for transfers between devices, local(): lax.psum((inner(whole_rows, whole_rows) / total, inner(whole_stiff, whole...  186 us
    all_gather x1, waiting for transfers between devices, local(): lax.all_gather(stiff, 'col', axis=0, tiled=True)  29 us
    ppermute x6, starting transfers between devices, shifted(): lax.ppermute(value, axis, [(source, source + steps) for source in range(i...  22 us
    dot_general x3, matrix products, apply_stiffness(): front = jnp.einsum('jsab,mjsb->mja', coupling, neighbours, precision=HIGH)  19.4 us
    dot_general x3, matrix products, apply_stiffness(): back = jnp.einsum('jsab,mja->mjsb', coupling, blocks, precision=HIGH)  15.3 us
    all_gather x1, waiting for transfers between devices, local(): lax.all_gather(filtered, 'col', axis=0, tiled=True)  14.2 us
    another operation x3, other arithmetic, local(): lower = jnp.linalg.cholesky(gram)  12.4 us
    another operation x2, other arithmetic, local(): jax.scipy.linalg.solve_triangular(lower, jnp.eye(full, dtype=jnp.float32)...  10.5 us
  transfers between devices with their start and end apart: 9, of which 5 were waited for; matrix products, arithmetic and copies ran while one was open for 8% of the time, Pallas kernels for 0%

commit v1 on v0

v1 whole, which is shorter than its diff:
```python
import functools

import jax
import jax.numpy as jnp
from jax import lax
from jax.experimental import pallas as pl
from jax.experimental.pallas import tpu as pltpu
from jax.sharding import PartitionSpec as P

HIGH = lax.Precision.HIGHEST
TILE = 96
LANES = 128
NBLK = 24
REACH = 3
COLS = 32
NCOL = 4
MESH = pl.DeviceIdType.MESH
F32 = jnp.float32
BF16 = jnp.bfloat16


def roll(x, shift):
    return pltpu.roll(x, shift, 1)


def lane_id(rows):
    return lax.broadcasted_iota(jnp.int32, (rows, LANES), 1)


def spread_lanes(x0, x1, x2):
    lane = lane_id(x0.shape[0])
    b1 = jnp.where(lane < 32, roll(x0, 32), roll(x1, 32))
    b2 = jnp.where(lane < 64, roll(x1, 64), roll(x2, 64))
    return x0, b1, b2, roll(x2, 96)


def pack_lanes(b0, b1, b2, b3):
    lane = lane_id(b0.shape[0])
    x0 = jnp.where(lane < 96, b0, roll(b1, 96))
    x1 = jnp.where(lane < 64, roll(b1, 96), roll(b2, 64))
    x2 = jnp.where(lane < 32, roll(b2, 64), roll(b3, 32))
    return x0, x1, x2


def halves(x):
    hi = x.astype(BF16)
    return hi, (x - hi.astype(F32)).astype(BF16)


def contract(left, right, dims, precision=None):
    return lax.dot_general(left, right, (dims, ((), ())), precision=precision, preferred_element_type=F32)


def filter_kernel(
    ntile, zc, block_ref, tiles_ref, mask_ref, adj_ref, diag_ref, low_ref, high_ref,
    rows_out, sums_out,
    tiles_v, merged, ph, plo, v0, v1, v2, vh, acc, ahead, spill, dense, stiff, part, rx1, rx2, sums,
    tile_sem, out_sem, ahead_send, ahead_recv, spill_send, spill_recv, x_send, x_recv, r_send, r_recv,
):
    tile = lax.axis_index("tile")
    col = lax.axis_index("col")
    ny = ntile // zc
    q = lax.rem(tile, zc)
    y = lax.div(tile, zc)
    following = lax.rem(tile + 1, ntile)
    previous = lax.rem(tile + ntile - 1, ntile)
    right = lax.rem(col + 1, NCOL)
    left = lax.rem(col + 3, NCOL)
    opposite = lax.rem(col + 2, NCOL)
    zpeers = [y * zc + lax.rem(q + d, zc) for d in range(1, zc)]
    ypeers = [lax.rem(y + d, ny) * zc + q for d in range(1, ny)]

    barrier = pltpu.get_barrier_semaphore()
    peers = [(t, col) for t in [following, previous] + zpeers + ypeers]
    peers += [(tile, c) for c in (right, left, opposite)]
    for peer in peers:
        pl.semaphore_signal(barrier, inc=1, device_id=peer, device_id_type=MESH)

    chunk = 6
    nchunk = NBLK // chunk
    per = 4 * 72

    def tile_copy(i):
        rows = pl.ds(i * chunk * per, chunk * per)
        return pltpu.make_async_copy(tiles_ref.at[rows], tiles_v.at[rows], tile_sem.at[i])

    for i in range(nchunk):
        tile_copy(i).start()

    valid32 = lane_id(COLS) < TILE
    for g in range(NBLK // 4):
        xs = [block_ref[:, pl.ds((3 * g + i) * LANES, LANES)] for i in range(3)]
        for i, piece in enumerate(spread_lanes(*xs)):
            piece = jnp.where(valid32, piece, 0.0)
            v0[4 * g + i] = piece
            hi, lo = halves(piece)
            vh[4 * g + i, 0:COLS] = hi
            vh[4 * g + i, COLS:2 * COLS] = lo

    valid24 = lane_id(24) < TILE

    def prepare(p, _):
        for par in range(2):
            j = 2 * p + par
            base = 128 * par
            marks = roll(mask_ref[...], 128 - 4 * j)
            slots = []
            for s in range(4):
                xs = [tiles_v[pl.ds(per * j + 4 * f + s, 24, stride=12), :] for f in range(3)]
                pieces = []
                for rho, piece in enumerate(spread_lanes(*xs)):
                    mark = jnp.broadcast_to(marks[24 * rho:24 * rho + 24, s:s + 1], (24, LANES))
                    pieces.append(jnp.where(valid24, piece * mark, 0.0))
                slots.append(pieces)
            for r in range(REACH):
                here = [jnp.where(adj_ref[4 * j + s] == r + 1, 1.0, 0.0).astype(F32) for s in range(4)]
                for rho in range(4):
                    total = slots[0][rho] * here[0]
                    for s in range(1, 4):
                        total += slots[s][rho] * here[s]
                    merged[par, r, pl.ds(rho, 24, stride=4), :] = total
            for r in range(REACH):
                hi, lo = halves(merged[par, r])
                lanes = pl.ds(LANES * (par + r), LANES)
                ph[p, base:base + TILE, lanes] = hi
                plo[p, base:base + TILE, lanes] = lo
            blank = pl.ds(3 * LANES * (1 - par), LANES)
            for ref in (ph, plo):
                ref[p, base:base + TILE, blank] = jnp.zeros((TILE, LANES), BF16)
                ref[p, base + TILE:base + LANES, :] = jnp.zeros((LANES - TILE, 4 * LANES), BF16)
        return 0

    for i in range(nchunk):
        tile_copy(i).wait()
        lax.fori_loop(i * chunk // 2, (i + 1) * chunk // 2, prepare, 0)

    pl.semaphore_wait(barrier, len(peers))

    has_next = tile < ntile - 1
    has_prev = tile > 0
    low = jnp.full((1, LANES), low_ref[0], F32)
    high = jnp.full((1, LANES), high_ref[0], F32)
    center = (low + high) / 2.0
    inv_half = 1.0 / ((high - low) / 2.0)

    def triple(lhs, hi, lo, dims):
        both = contract(lhs, hi, dims)
        return both[:COLS] + both[COLS:] + contract(lhs[:COLS], lo, dims)

    def back(p):
        lhs = jnp.concatenate([vh[2 * p], vh[2 * p + 1]], axis=1)
        res = triple(lhs, ph[p], plo[p], ((1,), (0,)))
        for t in range(4):
            acc[2 * p + 1 + t] += res[:, LANES * t:LANES * (t + 1)]

    def front(p):
        lhs = jnp.concatenate([vh[2 * p + 1 + t] for t in range(4)], axis=1)
        res = triple(lhs, ph[p], plo[p], ((1,), (1,)))
        for t in range(2):
            acc[2 * p + t] += res[:, LANES * t:LANES * (t + 1)]

    def both(p, _):
        back(p)
        front(p)
        return 0

    def apply(a, vec, finish, midway=None):
        to_prev = pltpu.make_async_remote_copy(
            src_ref=vec.at[pl.ds(0, REACH)], dst_ref=ahead.at[a], send_sem=ahead_send.at[a],
            recv_sem=ahead_recv.at[a], device_id=(previous, col), device_id_type=MESH)
        to_prev.start()
        for i in range(NBLK + REACH):
            acc[i] = jnp.zeros((COLS, LANES), F32)
        back(NBLK // 2 - 2)
        back(NBLK // 2 - 1)
        to_next = pltpu.make_async_remote_copy(
            src_ref=acc.at[pl.ds(NBLK, REACH)], dst_ref=spill.at[a], send_sem=spill_send.at[a],
            recv_sem=spill_recv.at[a], device_id=(following, col), device_id_type=MESH)
        to_next.start()
        lax.fori_loop(0, NBLK // 2 - 2, both, 0)
        if midway is not None:
            midway()
        to_prev.wait_recv()
        for i in range(REACH):
            hi, lo = halves(jnp.where(has_next, ahead[a, i], 0.0))
            vh[NBLK + i, 0:COLS] = hi
            vh[NBLK + i, COLS:2 * COLS] = lo
        front(NBLK // 2 - 2)
        front(NBLK // 2 - 1)
        to_next.wait_recv()
        for i in range(REACH):
            acc[i] += jnp.where(has_prev, spill[a, i], 0.0)
        to_prev.wait_send()
        to_next.wait_send()

        def step(i, _):
            finish(i, diag_ref[pl.ds(i, 1), :] * vec[i] - acc[i])
            return 0

        lax.fori_loop(0, NBLK, step, 0)

    def keep(i, value):
        hi, lo = halves(value)
        vh[i, 0:COLS] = hi
        vh[i, COLS:2 * COLS] = lo

    def finish_first(i, kv):
        value = (kv - center * v0[i]) * inv_half
        v1[i] = value
        keep(i, value)

    def finish_filtered(i, kv):
        value = 2.0 * ((kv - center * v1[i]) * inv_half) - v0[i]
        v2[i] = value
        keep(i, value)

    def finish_stiff(i, kv):
        v1[i] = kv

    apply(0, v0, finish_first)
    apply(1, v1, finish_filtered)

    def compact(src, put):
        for g in range(NBLK // 4):
            for i, x in enumerate(pack_lanes(*[src[4 * g + k] for k in range(4)])):
                put((3 * g + i) // 9, pl.ds((3 * g + i) % 9 * LANES, LANES), x)

    def put_dense(h, lanes, x):
        dense[col, h, :, lanes] = x

    def put_stiff(h, lanes, x):
        stiff[h, :, lanes] = x

    def x_copy(i, source, h, to):
        return pltpu.make_async_remote_copy(
            src_ref=dense.at[source, h], dst_ref=dense.at[source, h], send_sem=x_send.at[i],
            recv_sem=x_recv.at[i], device_id=(tile, to), device_id_type=MESH)

    compact(v2, put_dense)
    own = [x_copy(0, col, 0, right), x_copy(1, col, 1, left), x_copy(2, col, 1, right), x_copy(3, col, 0, left)]
    relay = [x_copy(4, left, 0, right), x_copy(5, right, 1, left)]
    for copy in own:
        copy.start()

    def pass_on():
        own[0].wait_recv()
        relay[0].start()
        own[1].wait_recv()
        relay[1].start()

    apply(2, v2, finish_stiff, pass_on)
    compact(v1, put_stiff)
    for copy in own[2:] + relay:
        copy.wait_recv()
    for copy in own + relay:
        copy.wait_send()

    to_out = pltpu.make_async_copy(dense, rows_out, out_sem)
    to_out.start()

    total = jnp.zeros((2 * COLS, LANES), F32)
    for h in range(2):
        lhs = jnp.concatenate([dense[col, h], stiff[h]], axis=0)
        rhs = jnp.concatenate([dense[c, h] for c in range(NCOL)], axis=0)
        total += contract(lhs, rhs, ((1,), (1,)), HIGH)
    total = total * (1.0 / (NBLK * TILE * ntile))

    share = 2 * COLS // zc
    for i in range(zc):
        part[i] = total[share * i:share * (i + 1)]

    def r_copy(i, src, dst, to):
        return pltpu.make_async_remote_copy(
            src_ref=src, dst_ref=dst, send_sem=r_send.at[i], recv_sem=r_recv.at[i],
            device_id=to, device_id_type=MESH)

    def arrived(i, ref):
        copy = r_copy(i, ref, ref, (tile, right))
        copy.wait_recv()
        copy.wait_send()

    for d in range(1, zc):
        r_copy(0, part.at[lax.rem(q + d, zc)], rx1.at[d - 1], (zpeers[d - 1], col)).start()
    arrived(0, rx1)
    mine = part[q]
    for d in range(zc - 1):
        mine += rx1[d]
    rx2[y] = mine
    for t in ypeers:
        r_copy(1, rx2.at[y], rx2.at[y], (t, col)).start()
    arrived(1, rx2.at[pl.ds(0, ny - 1)])
    mine = rx2[0]
    for i in range(1, ny):
        mine += rx2[i]
    sums[col, q] = mine
    for t in zpeers:
        r_copy(2, sums.at[col, q], sums.at[col, q], (t, col)).start()
    arrived(2, sums.at[0, pl.ds(0, zc - 1)])
    for c in (right, left, opposite):
        r_copy(3, sums.at[col], sums.at[col], (tile, c)).start()
    arrived(3, sums.at[pl.ds(0, NCOL - 1)])
    for c in range(NCOL):
        for i in range(zc):
            sums_out[c, share * i:share * (i + 1), :] = sums[c, i]
    to_out.wait()


def ritz_kernel(rows_ref, sums_ref, high_ref, basis_ref, reduced_ref, inv_ref):
    col = lax.axis_index("col")
    m = NCOL * COLS
    groups = m // 8
    lane = lax.broadcasted_iota(jnp.int32, (8, m), 1)
    sub = lax.broadcasted_iota(jnp.int32, (8, m), 0)
    a = [sums_ref[(8 * g) // COLS, pl.ds((8 * g) % COLS, 8), :] for g in range(groups)]
    pivots = []
    for g in range(groups):
        c = [[jnp.broadcast_to(a[h][:, 8 * g + t:8 * g + t + 1], (8, m)) for h in range(g, groups)] for t in range(8)]
        kept = jnp.ones((8, m), F32)
        for t in range(8):
            k = 8 * g + t
            pivot = jnp.broadcast_to(c[t][0][t:t + 1], (8, m))
            kept = jnp.where(sub == t, pivot, kept)
            inv = 1.0 / pivot
            row = jnp.where(lane == k, 1.0, jnp.broadcast_to(a[g][t:t + 1], (8, m)))
            facts = [x * inv for x in c[t]]
            facts[0] = jnp.where(sub > t, facts[0], 0.0)
            for u in range(t + 1, 8):
                same = jnp.broadcast_to(c[t][0][u:u + 1], (8, m))
                c[u] = [x - f * same for x, f in zip(c[u], facts)]
            for h in range(g, groups):
                old = jnp.where((lane == k) & (sub > t) if h == g else lane == k, 0.0, a[h])
                a[h] = old - facts[h - g] * row
        pivots.append(kept)
    for g in range(groups):
        row = sub + 8 * g
        unit = jnp.where(lane < row, a[g], jnp.where(lane == row, 1.0, 0.0))
        inv_ref[8 * g:8 * g + 8, :] = unit / jnp.sqrt(pivots[g])
    mine = inv_ref[pl.ds(col * COLS, COLS), :]
    for h in range(2):
        rhs = jnp.concatenate([rows_ref[c, h] for c in range(NCOL)], axis=0)
        width = rhs.shape[1]
        basis_ref[:, width * h:width * (h + 1)] = contract(mine, rhs, ((1,), (0,)), HIGH)
    inverse = inv_ref[...]
    proj = jnp.concatenate([sums_ref[c, COLS:2 * COLS] for c in range(NCOL)], axis=0)
    half = contract(inverse, proj, ((1,), (0,)), HIGH)
    reduced_ref[...] = contract(half, inverse, ((1,), (1,)), HIGH) / high_ref[0]


def local(ntile, block, tiles, intact, adjacency, stiff_diag, cut_low, cut_high):
    zc = min(16, ntile)
    ny = ntile // zc
    share = 2 * COLS // zc
    flat = tiles.reshape(NBLK, 4, 72, LANES).transpose(0, 2, 1, 3).reshape(NBLK * 4 * 72, LANES)
    mask = intact.astype(F32).reshape(NBLK * 4, 24, 4).transpose(2, 1, 0).reshape(TILE, NBLK * 4)
    mask = jnp.pad(mask, ((0, 0), (0, LANES - NBLK * 4)))
    diag = jnp.pad(stiff_diag.reshape(NBLK, TILE), ((0, 0), (0, LANES - TILE)))
    vm = pl.BlockSpec(memory_space=pltpu.VMEM)
    sm = pl.BlockSpec(memory_space=pltpu.SMEM)
    hbm = pl.BlockSpec(memory_space=pl.ANY)
    npair = NBLK // 2
    dma = pltpu.SemaphoreType.DMA
    vec = pltpu.VMEM((NBLK, COLS, LANES), F32)
    rows, sums = pl.pallas_call(
        functools.partial(filter_kernel, ntile, zc),
        out_shape=(
            jax.ShapeDtypeStruct((NCOL, 2, COLS, 1152), F32),
            jax.ShapeDtypeStruct((NCOL, 2 * COLS, LANES), F32),
        ),
        in_specs=[vm, hbm, vm, sm, vm, sm, sm],
        out_specs=(hbm, vm),
        scratch_shapes=[
            pltpu.VMEM((NBLK * 4 * 72, LANES), F32),
            pltpu.VMEM((2, REACH, TILE, LANES), F32),
            pltpu.VMEM((npair, 2 * LANES, 4 * LANES), BF16),
            pltpu.VMEM((npair, 2 * LANES, 4 * LANES), BF16),
            vec, vec, vec,
            pltpu.VMEM((NBLK + REACH, 2 * COLS, LANES), BF16),
            pltpu.VMEM((NBLK + REACH, COLS, LANES), F32),
            pltpu.VMEM((3, REACH, COLS, LANES), F32),
            pltpu.VMEM((3, REACH, COLS, LANES), F32),
            pltpu.VMEM((NCOL, 2, COLS, 1152), F32),
            pltpu.VMEM((2, COLS, 1152), F32),
            pltpu.VMEM((zc, share, LANES), F32),
            pltpu.VMEM((zc - 1, share, LANES), F32),
            pltpu.VMEM((ny, share, LANES), F32),
            pltpu.VMEM((NCOL, zc, share, LANES), F32),
            dma((4,)), dma, dma((3,)), dma((3,)), dma((3,)), dma((3,)),
            dma((6,)), dma((6,)), dma((4,)), dma((4,)),
        ],
        compiler_params=pltpu.CompilerParams(
            collective_id=0, has_side_effects=True, vmem_limit_bytes=48 * 1024 * 1024),
        name="filter",
    )(block, flat, mask, adjacency.reshape(NBLK * 4), diag, cut_low, cut_high)
    return pl.pallas_call(
        ritz_kernel,
        out_shape=(
            jax.ShapeDtypeStruct((COLS, NBLK * TILE), F32),
            jax.ShapeDtypeStruct((NCOL * COLS, NCOL * COLS), F32),
        ),
        in_specs=[vm, vm, sm],
        out_specs=(vm, vm),
        scratch_shapes=[pltpu.VMEM((NCOL * COLS, NCOL * COLS), F32)],
        compiler_params=pltpu.CompilerParams(vmem_limit_bytes=32 * 1024 * 1024),
        name="ritz",
    )(rows, sums, cut_high)


def solution(mesh):
    in_specs = (
        P("col", "tile"),
        P("tile", None, None),
        P("tile", None, None),
        P("tile", None),
        P("tile"),
        P(),
        P(),
    )
    out_specs = (P("col", "tile"), P())
    return jax.shard_map(
        functools.partial(local, mesh.shape["tile"]), mesh=mesh, in_specs=in_specs, out_specs=out_specs,
        check_vma=False)
```

time: 356 us -> 73.4 us (0.21)
  waiting for transfers between devices: 230 us -> 0 us
  Pallas kernels: 0 us -> 65.7 us
  matrix products: 49.6 us -> 0 us
  other arithmetic: 24.8 us -> 0.81 us
  starting transfers between devices: 22.3 us -> 0 us
  between operations: 15.5 us -> 1.96 us
  local copies, waits for them, and re-layouts: 13.3 us -> 4.59 us
    psum x1 -> x0, waiting for transfers between devices: 186 us -> none  [local(): lax.psum((inner(whole_rows, whole_rows) / total, inner(whole_stiff, whole...]
    pallas_call x0 -> x2, Pallas kernels: none -> 65.7 us  [the longest x1 59.9 us: local(): pl.pallas_call(functools.partial(filter_kernel, ntile, zc), out_shape=(ja...]
    dot_general x14 -> x0, matrix products: 49.4 us -> none  [the longest x3 19.4 us: apply_stiffness(): front = jnp.einsum('jsab,mjsb->mja', coupling, neighbours, precision=HIGH)]
    all_gather x2 -> x0, waiting for transfers between devices: 43.2 us -> none  [the longest x1 29 us: local(): lax.all_gather(stiff, 'col', axis=0, tiled=True)]
    another operation x5 -> x0, other arithmetic: 22.9 us -> none  [the longest x3 12.4 us: local(): lower = jnp.linalg.cholesky(gram)]
    ppermute x6 -> x0, starting transfers between devices: 22 us -> none  [shifted(): lax.ppermute(value, axis, [(source, source + steps) for source in range(i...]
    reshape x10 -> x3, local copies, waits for them, and re-layouts: 7.35 us -> 1.26 us  [the longest x1 0.78 us: local(): diag = jnp.pad(stiff_diag.reshape(NBLK, TILE), ((0, 0), (0, LANES - TILE)))]
  transfers between devices with their start and end apart: 9 -> 0, of which waited for: 5 -> 0; matrix products, arithmetic and copies ran while one was open for 8% -> 0% of each run, Pallas kernels for 0% -> 0%
where the time goes in v1:
time: 73.4 us; the launch traced here: 73.1 us
  Pallas kernels  65.7 us (90%)
  local copies, waits for them, and re-layouts  4.59 us (6%)
  between operations  1.96 us (3%)
  other arithmetic  0.81 us (1%)
    pallas_call x1, Pallas kernels, local(): pl.pallas_call(functools.partial(filter_kernel, ntile, zc), out_shape=(ja...  59.9 us
    pallas_call x1, Pallas kernels, local(): pl.pallas_call(ritz_kernel, out_shape=(jax.ShapeDtypeStruct((COLS, NBLK *...  5.86 us
    unnamed x5, local copies, waits for them, and re-layouts  2.9 us

profile of v1, /device:TPU:1, one launch (start us, length us, event | category | flops | bytes accessed | tf_op | source)
XLA Modules:
  0.0 73.1 jit_solution(13295983487371564510)
XLA Ops:
  1.9 0.8 %copy.14 = s32[24,4]{1,0:T(8,128)S(1)} copy(s32[24,4]{0,1:T(4,128)} %param.10) | data formatting | bytes 768 | tf_op args[3]
  2.7 0.1 reshape.26.adj_ref
  2.8 0.8 %reshape.27 = f32[24,96]{1,0:T(8,128)S(1)} reshape(f32[2304]{0:T(1024)} %param.11) | data formatting | bytes 18432 | tf_op jit(solution)/shard_map/reshape | solution.py:356
  3.6 0.8 %convert_element_type.7 = f32[24,4,96]{2,1,0:T(4,128)S(1)} convert(s32[24,4,96]{2,1,0:T(4,128)} %param.9) | non-fusion elementwise | flops 9216 | bytes 73728 | tf_op jit(solution)/shard_map/convert_element_type | solution.py:354
  4.4 0.0 copy-start.1
  4.4 0.4 reshape.24
  4.8 0.4 copy.13
  5.2 0.1 copy-done.1
  5.3 0.0 copy-start
  5.3 2.0 %copy-done = f32[24,4,9216]{2,1,0:T(4,128)S(1)} copy-done((f32[24,4,9216]{2,1,0:T(4,128)S(1)}, f32[24,4,9216]{2,1,0:T(4,128)}, u32[]{:S(2)}) %copy-start) | copy-done | bytes 3538968
  7.3 59.9 %filter.1 = (f32[4,2,32,1152]{3,2,1,0:T(8,128)S(1)}, f32[4,64,128]{2,1,0:T(8,128)S(1)}) custom-call(f32[32,2304]{1,0:T(8,128)S(1)} %copy-done.1, f32[6912,128]{1,0:T(8,128)S(1)} %bitcast.7, f32[96,128]{1,0:T(8,128)S(1)} %pad.8.mask_ref, s32[96]{0:T(128)S(1)} %reshape.26.adj_ref, f32[24,128]{1,0:T(8,128)S(1)} %pad.9.diag_ref, f32[1]{0:T(128)S(6)} %copy.15.low_ref, ...), custom_call_target="tpu_custom_call" | custom-call | tf_op jit(solution)/shard_map/filter/pallas_call | solution.py:363
  67.2 5.9 %ritz.1 = (f32[32,2304]{1,0:T(8,128)}, f32[128,128]{1,0:T(8,128)}) custom-call(f32[4,2,32,1152]{3,2,1,0:T(8,128)S(1)} %get-tuple-element.4.rows_ref, f32[4,64,128]{2,1,0:T(8,128)S(1)} %get-tuple-element.5.sums_ref, f32[1]{0:T(128)S(6)} %copy.16.high_ref), custom_call_target="tpu_custom_call" | custom-call | tf_op jit(solution)/shard_map/ritz/pallas_call | solution.py:394
  (2 shorter events, 0.0 us)
Async XLA Ops:
  4.4 1.0 %copy-start.1 = (f32[32,2304]{1,0:T(8,128)S(1)}, f32[32,2304]{1,0:T(8,128)}, u32[]{:S(2)}) copy-start(f32[32,2304]{1,0:T(8,128)} %block_ref.1) | copy-start | bytes 884740
  5.3 2.0 %copy-start = (f32[24,4,9216]{2,1,0:T(4,128)S(1)}, f32[24,4,9216]{2,1,0:T(4,128)}, u32[]{:S(2)}) copy-start(f32[24,4,9216]{2,1,0:T(4,128)} %param.8) | copy-start | bytes 10616836

commit v2 on v0

v2 whole, which is shorter than its diff:
```python
import functools

import jax
import jax.numpy as jnp
from jax import lax
from jax.experimental import pallas as pl
from jax.experimental.pallas import tpu as pltpu
from jax.sharding import PartitionSpec as P

HIGH = lax.Precision.HIGHEST
TILE = 96
LANES = 128
NBLK = 24
REACH = 3
COLS = 32
NCOL = 4
MESH = pl.DeviceIdType.MESH
F32 = jnp.float32
BF16 = jnp.bfloat16


def aligned(x, step):
    return x if isinstance(x, int) else pl.multiple_of(x, step)


def roll(x, shift):
    return pltpu.roll(x, shift, 1)


def lane_id(rows):
    return lax.broadcasted_iota(jnp.int32, (rows, LANES), 1)


def spread_lanes(x0, x1, x2):
    lane = lane_id(x0.shape[0])
    b1 = jnp.where(lane < 32, roll(x0, 32), roll(x1, 32))
    b2 = jnp.where(lane < 64, roll(x1, 64), roll(x2, 64))
    return x0, b1, b2, roll(x2, 96)


def pack_lanes(b0, b1, b2, b3):
    lane = lane_id(b0.shape[0])
    x0 = jnp.where(lane < 96, b0, roll(b1, 96))
    x1 = jnp.where(lane < 64, roll(b1, 96), roll(b2, 64))
    x2 = jnp.where(lane < 32, roll(b2, 64), roll(b3, 32))
    return x0, x1, x2


def halves(x):
    hi = x.astype(BF16)
    return hi, (x - hi.astype(F32)).astype(BF16)


def contract(left, right, dims, precision=None):
    return lax.dot_general(left, right, (dims, ((), ())), precision=precision, preferred_element_type=F32)


def ritz(col, rows_ref, sums_ref, high_ref, basis_ref, reduced_ref, inv_ref):
    m = NCOL * COLS
    groups = m // 8
    lane = lax.broadcasted_iota(jnp.int32, (8, m), 1)
    sub = lax.broadcasted_iota(jnp.int32, (8, m), 0)
    a = [sums_ref[8 * (g // 4) + g % 4] for g in range(groups)]
    pivots = []
    for g in range(groups):
        c = [[jnp.broadcast_to(a[h][:, 8 * g + t:8 * g + t + 1], (8, m)) for h in range(g, groups)] for t in range(8)]
        kept = jnp.ones((8, m), F32)
        for t in range(8):
            k = 8 * g + t
            pivot = jnp.broadcast_to(c[t][0][t:t + 1], (8, m))
            kept = jnp.where(sub == t, pivot, kept)
            inv = 1.0 / pivot
            row = jnp.where(lane == k, 1.0, jnp.broadcast_to(a[g][t:t + 1], (8, m)))
            facts = [x * inv for x in c[t]]
            facts[0] = jnp.where(sub > t, facts[0], 0.0)
            for u in range(t + 1, 8):
                same = jnp.broadcast_to(c[t][0][u:u + 1], (8, m))
                c[u] = [x - f * same for x, f in zip(c[u], facts)]
            for h in range(g, groups):
                old = jnp.where((lane == k) & (sub > t) if h == g else lane == k, 0.0, a[h])
                a[h] = old - facts[h - g] * row
        pivots.append(kept)
    for g in range(groups):
        row = sub + 8 * g
        unit = jnp.where(lane < row, a[g], jnp.where(lane == row, 1.0, 0.0))
        inv_ref[8 * g:8 * g + 8, :] = unit / jnp.sqrt(pivots[g])
    mine = inv_ref[pl.ds(col * COLS, COLS), :]
    mine = jnp.concatenate(halves(mine), axis=0)
    for g in range(NBLK // 4):
        hi, lo = halves(jnp.concatenate([rows_ref[c, g] for c in range(NCOL)], axis=0))
        width = hi.shape[1]
        both = contract(mine, hi, ((1,), (0,)))
        low = contract(mine[:COLS], lo, ((1,), (0,)))
        basis_ref[:, width * g:width * (g + 1)] = both[:COLS] + (both[COLS:] + low)
    inverse = inv_ref[...]
    proj = jnp.concatenate([sums_ref[8 * (g // 4) + 4 + g % 4] for g in range(groups)], axis=0)
    half = contract(inverse, proj, ((1,), (0,)), HIGH)
    reduced_ref[...] = contract(half, inverse, ((1,), (1,)), HIGH) / high_ref[0]


def filter_kernel(
    ntile, zc, block_ref, tiles_ref, intact_ref, adj_ref, diag_ref, low_ref, high_ref,
    basis_ref, reduced_ref,
    tiles_v, intact_v, block_v, diag_in, marks_k, marks_f, marks_in, marks_v, diag_v, merged, qh, qlo, v0, v1, v2, vh, ahead, spill, spill_out, dense, stiff,
    part, rx1, rx2, sums, inv_v,
    tile_sem, in_sem, ahead_send, ahead_recv, spill_send, spill_recv, x_send, x_recv, r_send, r_recv,
):
    tile = lax.axis_index("tile")
    col = lax.axis_index("col")
    ny = ntile // zc
    q = lax.rem(tile, zc)
    y = lax.div(tile, zc)
    following = lax.rem(tile + 1, ntile)
    previous = lax.rem(tile + ntile - 1, ntile)
    right = lax.rem(col + 1, NCOL)
    left = lax.rem(col + 3, NCOL)
    opposite = lax.rem(col + 2, NCOL)
    zpeers = [(y * zc + lax.rem(q + d, zc), col) for d in range(1, zc)]
    ypeers = [(lax.rem(y + d, ny) * zc + q, col) for d in range(1, ny)]
    core = lax.rem(q, 2)

    def near(dz, c, other):
        return (y * zc + lax.rem(q - core + 2 * dz + zc, zc) + (1 - core if other else core), c)

    spread = [near(dz, c, other) for c in (col, right, left, opposite) for dz in (0, 1, -1, -2)
              for other in (False, True)][1:]

    barrier = pltpu.get_barrier_semaphore()
    peers = [(following, col), (previous, col)] + ypeers + zpeers
    peers += [near(dz, c, other) for c in (right, left, opposite) for dz in (-2, -1, 0, 1, 2)
              for other in (False, True)]

    npair = NBLK // 2
    per = 4 * 72
    chunk = 3

    def tile_copy(i):
        rows = pl.ds(i * 2 * chunk * per, 2 * chunk * per)
        return pltpu.make_async_copy(tiles_ref.at[rows], tiles_v.at[rows], tile_sem.at[i])

    order = (3, 0, 1, 2)
    small = [pltpu.make_async_copy(src, dst, in_sem.at[i]) for i, (src, dst) in enumerate(
        ((intact_ref, intact_v), (block_ref, block_v), (diag_ref, diag_in)))]
    for copy in small:
        copy.start()
    for i in order:
        tile_copy(i).start()
    for peer in peers:
        pl.semaphore_signal(barrier, inc=1, device_id=peer, device_id_type=MESH)

    def window(buf, p, first=0, last=8):
        start = aligned(2 * LANES * p + LANES * first, LANES)
        return vh[buf, :, pl.ds(start, LANES * (last - first))]

    def keep(buf, p, value):
        hi, lo = halves(value)
        lanes = pl.ds(aligned(2 * LANES * p + REACH * LANES, LANES), value.shape[1])
        vh[buf, 0:COLS, lanes] = hi
        vh[buf, COLS:2 * COLS, lanes] = lo

    def pair(p):
        return pl.ds(aligned(2 * LANES * p, 2 * LANES), 2 * LANES)

    merged[...] = jnp.zeros(merged.shape, F32)
    for ref in (qh, qlo):
        for p, w, c in ((0, 0, 0), (0, 1, 0), (0, 2, 0), (0, 1, 1), (0, 2, 1), (1, 0, 0), (npair, 0, 1)):
            ref[p, pl.ds(LANES * w, LANES), pl.ds(LANES * c, LANES)] = jnp.zeros((LANES, LANES), BF16)
    for buf in range(2):
        vh[buf, :, 0:REACH * LANES] = jnp.zeros((2 * COLS, REACH * LANES), BF16)

    nmark = 3 * 4 * LANES
    rows_id = lax.broadcasted_iota(jnp.int32, (16, nmark), 0)
    lanes_id = lax.broadcasted_iota(jnp.int32, (16, nmark), 1)
    slot_at = lax.div(lanes_id, 3 * LANES)
    row_at = lax.div(lax.rem(lanes_id, 3 * LANES), TILE)
    pick = jnp.where(rows_id == 4 * row_at + slot_at, 1.0, 0.0).astype(BF16)
    marks_in[...] = jnp.zeros((LANES, LANES), F32)
    small[0].wait()
    for j in range(NBLK):
        marks_in[4 * j:4 * j + 4, 0:TILE] = intact_v[j].astype(F32)
    marks_v[...] = marks_in[...].T
    lane24 = lane_id(24)

    def gather_marks(j, _):
        total = jnp.zeros((24, LANES), F32)
        for rho in range(4):
            moved = roll(marks_v[pl.ds(rho, 24, stride=4), :], lax.rem(LANES + 4 * rho - 4 * j, LANES))
            total = jnp.where((lane24 >= 4 * rho) & (lane24 < 4 * rho + 4), moved, total)
        marks_k[pl.ds(pl.multiple_of(24 * j, 8), 24), :] = total
        return 0

    lax.fori_loop(0, NBLK, gather_marks, 0, unroll=4)

    def spread_marks(i, _):
        rows = pl.ds(pl.multiple_of(96 * i, 8), 96)
        marks_f[rows, :] = contract(marks_k[rows, 0:16].astype(BF16), pick, ((1,), (0,)))
        return 0

    lax.fori_loop(0, 6, spread_marks, 0, unroll=2)

    small[1].wait()
    valid32 = lane_id(COLS) < TILE
    for g in range(NBLK // 4):
        xs = [block_v[:, pl.ds((3 * g + i) * LANES, LANES)] for i in range(3)]
        for i, piece in enumerate(spread_lanes(*xs)):
            piece = jnp.where(valid32, piece, 0.0)
            v0[:, pl.ds((4 * g + i) * LANES, LANES)] = piece
            hi, lo = halves(piece)
            lanes = pl.ds((4 * g + i + REACH) * LANES, LANES)
            vh[0, 0:COLS, lanes] = hi
            vh[0, COLS:2 * COLS, lanes] = lo
    small[2].wait()
    xs = [diag_in[pl.ds(i, NBLK // 4, stride=3), :] for i in range(3)]
    for i, piece in enumerate(spread_lanes(*xs)):
        diag_v[pl.ds(i, NBLK // 4, stride=4), :] = piece

    pl.semaphore_wait(barrier, len(peers))

    def ahead_copy(a, vec):
        return pltpu.make_async_remote_copy(
            src_ref=vec.at[:, pl.ds(0, REACH * LANES)], dst_ref=ahead.at[a], send_sem=ahead_send.at[a],
            recv_sem=ahead_recv.at[a], device_id=(previous, col), device_id_type=MESH)

    ahead_copy(0, v0).start()

    valid24 = lane_id(24) < TILE

    def prepare(p):
        for par in range(2):
            j = 2 * p + par
            rows = pl.ds(24 * j, 24)
            slots = []
            for s in range(4):
                xs = [tiles_v[pl.ds(per * j + 4 * f + s, 24, stride=12), :] for f in range(3)]
                slots.append([x * marks_f[rows, pl.ds((3 * s + f) * LANES, LANES)] for f, x in enumerate(xs)])
            for r in range(REACH):
                here = [jnp.where(adj_ref[s, j] == r + 1, 1.0, 0.0).astype(F32) for s in range(4)]
                xs = []
                for f in range(3):
                    xs.append((slots[0][f] * here[0] + slots[1][f] * here[1])
                              + (slots[2][f] * here[2] + slots[3][f] * here[3]))
                for rho, piece in enumerate(spread_lanes(*xs)):
                    merged[par, r, pl.ds(rho, 24, stride=4), :] = jnp.where(valid24, piece, 0.0)
            for r in range(REACH):
                value = merged[par, r]
                target = par + r + 1
                back_rows = pl.ds(LANES * (par + 3 - 2 * (target // 2)), LANES)
                back_lanes = pl.ds(LANES * (target % 2), LANES)
                hi, lo = halves(value)
                qh[p + target // 2, back_rows, back_lanes] = hi
                qlo[p + target // 2, back_rows, back_lanes] = lo
                front_rows = pl.ds(LANES * (target + 3), LANES)
                hi, lo = halves(value.T)
                qh[p, front_rows, pl.ds(LANES * par, LANES)] = hi
                qlo[p, front_rows, pl.ds(LANES * par, LANES)] = lo
        for ref in (qh, qlo):
            for w, c in ((3, 0), (7, 0), (0, 1), (4, 1)):
                ref[p, pl.ds(LANES * w, LANES), pl.ds(LANES * c, LANES)] = jnp.zeros((LANES, LANES), BF16)

    has_next = tile < ntile - 1
    has_prev = tile > 0
    low = jnp.full((1, 2 * LANES), low_ref[0], F32)
    high = jnp.full((1, 2 * LANES), high_ref[0], F32)
    center = (low + high) / 2.0
    inv_half = 1.0 / ((high - low) / 2.0)

    def product(lhs, hi, lo):
        both = contract(lhs, hi, ((1,), (0,)))
        return both[:COLS] + both[COLS:] + contract(lhs[:COLS], lo, ((1,), (0,)))

    def couple(buf, p, first=0, last=8):
        rows = pl.ds(LANES * first, LANES * (last - first))
        return product(window(buf, p, first, last), qh[p, rows, :], qlo[p, rows, :])

    def spill_copy(a):
        return pltpu.make_async_remote_copy(
            src_ref=spill_out.at[a], dst_ref=spill.at[a], send_sem=spill_send.at[a],
            recv_sem=spill_recv.at[a], device_id=(following, col), device_id_type=MESH)

    def send_spill(a, buf):
        spill_out[a, :, 0:2 * LANES] = couple(buf, npair, 0, 3)
        tail = window(buf, npair, 1, 3)[:, LANES:2 * LANES]
        spill_out[a, :, 2 * LANES:3 * LANES] = product(
            tail, qh[npair + 1, 0:LANES, 0:LANES], qlo[npair + 1, 0:LANES, 0:LANES])
        spill_copy(a).start()

    def stiffness(vec, p, res):
        lanes = pair(p)
        d = jnp.concatenate([diag_v[pl.ds(2 * p, 1), :], diag_v[pl.ds(2 * p + 1, 1), :]], axis=1)
        return d * vec[:, lanes] - res

    def inside(buf, vec, finish, p):
        finish(p, stiffness(vec, p, couple(buf, p)))
        return 0

    def apply(a, buf, vec, finish, hook=None, first=2):
        lax.fori_loop(first, npair - 2, lambda p, _: inside(buf, vec, finish, p), 0, unroll=2)
        if hook is not None:
            hook()
        heads = [couple(buf, p) for p in (0, 1)]
        tails = [couple(buf, npair - 2, 0, 6), couple(buf, npair - 1, 0, 4)]
        ahead_copy(a, vec).wait_recv()
        keep(buf, npair, jnp.where(has_next, ahead[a], 0.0))
        tails[0] += couple(buf, npair - 2, 6, 8)
        tails[1] += couple(buf, npair - 1, 4, 8)
        for i in range(2):
            finish(npair - 2 + i, stiffness(vec, npair - 2 + i, tails[i]))
        spill_copy(a).wait_recv()
        extra = jnp.where(has_prev, spill[a], 0.0)
        heads[0] += extra[:, 0:2 * LANES]
        heads[1] += jnp.concatenate([extra[:, 2 * LANES:], jnp.zeros((COLS, LANES), F32)], axis=1)
        for i in range(2):
            finish(i, stiffness(vec, i, heads[i]))
        ahead_copy(a, vec).wait_send()
        spill_copy(a).wait_send()

    def finish_first(p, kv):
        lanes = pair(p)
        value = (kv - center * v0[:, lanes]) * inv_half
        v1[:, lanes] = value
        keep(1, p, value)

    def finish_filtered(p, kv):
        lanes = pair(p)
        value = 2.0 * ((kv - center * v1[:, lanes]) * inv_half) - v0[:, lanes]
        v2[:, lanes] = value
        keep(0, p, value)

    def finish_stiff(p, kv):
        v1[:, pair(p)] = kv

    def compact(src, g):
        return pack_lanes(*[src[:, pl.ds((4 * g + k) * LANES, LANES)] for k in range(4)])

    ngroup = NBLK // 4
    lower = (0, 1, 2)
    upper = (3, 4, 5)

    def x_copy(i, source, g, to):
        return pltpu.make_async_remote_copy(
            src_ref=dense.at[source, g], dst_ref=dense.at[source, g], send_sem=x_send.at[i],
            recv_sem=x_recv.at[i], device_id=(tile, to), device_id_type=MESH)

    def to_right(g, source=None):
        if source is None:
            return x_copy(g, col, g, right)
        return x_copy(2 * ngroup + g, source, g, right)

    def to_left(g, source=None):
        if source is None:
            return x_copy(ngroup + g, col, g, left)
        return x_copy(2 * ngroup + g, source, g, left)

    def send_groups(rights, lefts):
        for g in sorted(set(rights + lefts)):
            for i, x in enumerate(compact(v2, g)):
                dense[col, g, :, LANES * i:LANES * (i + 1)] = x
        for a, b in zip(rights, lefts):
            to_right(a).start()
            to_left(b).start()

    for n, i in enumerate(order):
        tile_copy(i).wait()
        for p in range(i * chunk, (i + 1) * chunk):
            prepare(p)
            if 2 < p < npair - chunk:
                inside(0, v0, finish_first, p - 1)
        if n == 0:
            send_spill(0, 0)
    apply(0, 0, v0, finish_first, first=npair - chunk - 1)
    ahead_copy(1, v1).start()
    send_spill(1, 1)
    apply(1, 1, v1, finish_filtered, lambda: send_groups((1, 2, 3, 4), (4, 3, 2, 1)))
    ahead_copy(2, v2).start()
    send_spill(2, 0)
    send_groups((0, 5), (5, 0))

    def pass_on():
        for a, b in ((1, 4), (2, 3), (0, 5)):
            to_right(a).wait_recv()
            to_right(a, left).start()
            to_left(b).wait_recv()
            to_left(b, right).start()

    apply(2, 0, v2, finish_stiff)
    pass_on()
    for g in range(ngroup):
        for i, x in enumerate(compact(v1, g)):
            stiff[g, :, LANES * i:LANES * (i + 1)] = x

    def split_rows(g):
        hi_f, lo_f = halves(dense[col, g])
        hi_s, lo_s = halves(stiff[g])
        return jnp.concatenate([hi_f, hi_s, lo_f, lo_s], axis=0)

    own = [split_rows(g) for g in range(ngroup)]

    def against(source, groups):
        lhs = jnp.concatenate([own[g] for g in groups], axis=1)
        parts = [halves(dense[source, g]) for g in groups]
        rhs = jnp.concatenate([jnp.concatenate([x[i] for x in parts], axis=1) for i in range(2)], axis=0)
        res = contract(lhs, rhs, ((1,), (1,)))
        half = 2 * COLS
        return res[:half, :COLS] + res[half:, :COLS] + (res[:half, COLS:] + res[half:, COLS:])

    mine = against(col, lower + upper)
    of_left = against(left, lower)
    of_right = against(right, upper)
    for g in upper:
        to_right(g).wait_recv()
    of_left += against(left, upper)
    for g in lower:
        to_left(g).wait_recv()
    of_right += against(right, lower)
    of_opposite = jnp.zeros((2 * COLS, COLS), F32)
    for groups in ((1, 2, 3, 4), (0, 5)):
        for g in groups:
            (to_right(g, left) if g in lower else to_left(g, right)).wait_recv()
        of_opposite += against(opposite, groups)
    total = jnp.concatenate([mine, of_right, of_opposite, of_left], axis=1)
    total = roll(total, COLS * col) * (1.0 / (NBLK * TILE * ntile))

    nshare = 8
    share = 2 * COLS // nshare
    for i in range(nshare):
        part[i] = total[share * i:share * (i + 1)]

    def r_copy(i, src, dst, to):
        return pltpu.make_async_remote_copy(
            src_ref=src, dst_ref=dst, send_sem=r_send.at[i], recv_sem=r_recv.at[i],
            device_id=to, device_id_type=MESH)

    def arrived(i, ref):
        copy = r_copy(i, ref, ref, (tile, right))
        copy.wait_recv()
        copy.wait_send()

    for d in range(1, zc):
        r_copy(0, part.at[lax.rem(q + d, nshare)], rx1.at[q], zpeers[d - 1]).start()
    own_share = lax.rem(q, nshare)
    rx1[q] = part[own_share]
    arrived(0, rx1.at[pl.ds(0, zc - 1)])
    mine = rx1[0]
    for i in range(1, zc):
        mine += rx1[i]
    rx2[y] = mine
    for peer in ypeers:
        r_copy(1, rx2.at[y], rx2.at[y], peer).start()
    arrived(1, rx2.at[pl.ds(0, ny - 1)])
    mine = rx2[0]
    for i in range(1, ny):
        mine += rx2[i]
    here = nshare * col + own_share
    sums[here] = mine
    for peer in spread:
        r_copy(2, sums.at[here], sums.at[here], peer).start()
    arrived(2, sums.at[pl.ds(0, NCOL * nshare - 1)])
    for g in range(ngroup):
        to_right(g).wait_send()
        to_left(g).wait_send()
        (to_right(g, left) if g in lower else to_left(g, right)).wait_send()
    ritz(col, dense, sums, high_ref, basis_ref, reduced_ref, inv_v)


def local(ntile, block, tiles, intact, adjacency, stiff_diag, cut_low, cut_high):
    zc = min(16, ntile)
    ny = ntile // zc
    share = 2 * COLS // 8
    flat = tiles.reshape(NBLK, 4, 72, LANES).transpose(0, 2, 1, 3).reshape(NBLK * 4 * 72, LANES)
    diag = stiff_diag.reshape(NBLK * TILE // LANES, LANES)
    vm = pl.BlockSpec(memory_space=pltpu.VMEM)
    sm = pl.BlockSpec(memory_space=pltpu.SMEM)
    hbm = pl.BlockSpec(memory_space=pltpu.HBM)
    npair = NBLK // 2
    dma = pltpu.SemaphoreType.DMA
    vec = pltpu.VMEM((COLS, NBLK * LANES), F32)
    halo = pltpu.VMEM((3, COLS, REACH * LANES), F32)
    width = 4 * TILE
    return pl.pallas_call(
        functools.partial(filter_kernel, ntile, zc),
        out_shape=(
            jax.ShapeDtypeStruct((COLS, NBLK * TILE), F32),
            jax.ShapeDtypeStruct((NCOL * COLS, NCOL * COLS), F32),
        ),
        in_specs=[hbm, hbm, hbm, sm, hbm, sm, sm],
        out_specs=(vm, vm),
        scratch_shapes=[
            pltpu.VMEM((NBLK * 4 * 72, LANES), F32),
            pltpu.VMEM((NBLK, 4, TILE), jnp.int32),
            pltpu.VMEM((COLS, NBLK * TILE), F32),
            pltpu.VMEM((NBLK * TILE // LANES, LANES), F32),
            pltpu.VMEM((NBLK * 24, LANES), F32),
            pltpu.VMEM((NBLK * 24, 12 * LANES), F32),
            pltpu.VMEM((LANES, LANES), F32),
            pltpu.VMEM((LANES, LANES), F32),
            pltpu.VMEM((NBLK, LANES), F32),
            pltpu.VMEM((2, REACH, LANES, LANES), F32),
            pltpu.VMEM((npair + 2, 8 * LANES, 2 * LANES), BF16),
            pltpu.VMEM((npair + 2, 8 * LANES, 2 * LANES), BF16),
            vec, vec, vec,
            pltpu.VMEM((2, 2 * COLS, (NBLK + 2 * REACH) * LANES), BF16),
            halo, halo, halo,
            pltpu.VMEM((NCOL, NBLK // 4, COLS, width), F32),
            pltpu.VMEM((NBLK // 4, COLS, width), F32),
            pltpu.VMEM((8, share, LANES), F32),
            pltpu.VMEM((zc, share, LANES), F32),
            pltpu.VMEM((ny, share, LANES), F32),
            pltpu.VMEM((8 * NCOL, share, LANES), F32),
            pltpu.VMEM((NCOL * COLS, NCOL * COLS), F32),
            dma((4,)), dma((3,)), dma((3,)), dma((3,)), dma((3,)), dma((3,)),
            dma((18,)), dma((18,)), dma((3,)), dma((3,)),
        ],
        compiler_params=pltpu.CompilerParams(
            collective_id=0, has_side_effects=True, vmem_limit_bytes=57 * 1024 * 1024),
        name="filter",
    )(block, flat, intact, adjacency.T, diag, cut_low, cut_high)

def solution(mesh):
    in_specs = (
        P("col", "tile"),
        P("tile", None, None),
        P("tile", None, None),
        P("tile", None),
        P("tile"),
        P(),
        P(),
    )
    out_specs = (P("col", "tile"), P())
    return jax.shard_map(
        functools.partial(local, mesh.shape["tile"]), mesh=mesh, in_specs=in_specs, out_specs=out_specs,
        check_vma=False)
```

time: 356 us -> 63.7 us (0.18)
  waiting for transfers between devices: 230 us -> 0 us
  Pallas kernels: 0 us -> 58.4 us
  matrix products: 49.6 us -> 0 us
  other arithmetic: 24.8 us -> 0 us
  starting transfers between devices: 22.3 us -> 0 us
  between operations: 15.5 us -> 1.93 us
  local copies, waits for them, and re-layouts: 13.3 us -> 3.17 us
    psum x1 -> x0, waiting for transfers between devices: 186 us -> none  [local(): lax.psum((inner(whole_rows, whole_rows) / total, inner(whole_stiff, whole...]
    pallas_call x0 -> x1, Pallas kernels: none -> 58.4 us  [local(): pl.pallas_call(functools.partial(filter_kernel, ntile, zc), out_shape=(ja...]
    dot_general x14 -> x0, matrix products: 49.4 us -> none  [the longest x3 19.4 us: apply_stiffness(): front = jnp.einsum('jsab,mjsb->mja', coupling, neighbours, precision=HIGH)]
    all_gather x2 -> x0, waiting for transfers between devices: 43.2 us -> none  [the longest x1 29 us: local(): lax.all_gather(stiff, 'col', axis=0, tiled=True)]
    another operation x5 -> x0, other arithmetic: 22.9 us -> none  [the longest x3 12.4 us: local(): lower = jnp.linalg.cholesky(gram)]
    ppermute x6 -> x0, starting transfers between devices: 22 us -> none  [shifted(): lax.ppermute(value, axis, [(source, source + steps) for source in range(i...]
    reshape x10 -> x0, local copies, waits for them, and re-layouts: 7.35 us -> none  [the longest x1 5.89 us: local(): tiles.reshape(nblk, slots, width, width)]
  transfers between devices with their start and end apart: 9 -> 0, of which waited for: 5 -> 0; matrix products, arithmetic and copies ran while one was open for 8% -> 0% of each run, Pallas kernels for 0% -> 0%
where the time goes in v2:
time: 63.7 us; the launch traced here: 63.5 us
  Pallas kernels  58.4 us (92%)
  local copies, waits for them, and re-layouts  3.17 us (5%)
  between operations  1.93 us (3%)
    pallas_call x1, Pallas kernels, local(): pl.pallas_call(functools.partial(filter_kernel, ntile, zc), out_shape=(ja...  58.4 us
    unnamed x2, local copies, waits for them, and re-layouts  3.17 us

profile of v2, /device:TPU:1, one launch (start us, length us, event | category | flops | bytes accessed | tf_op | source)
XLA Modules:
  0.0 63.5 jit_solution(5088243856361718981)
XLA Ops:
  1.9 58.4 %filter.1 = (f32[32,2304]{1,0:T(8,128)}, f32[128,128]{1,0:T(8,128)}) custom-call(f32[32,2304]{1,0:T(8,128)} %block_ref.1, f32[6912,128]{1,0:T(8,128)} %bitcast.7, s32[24,4,96]{2,1,0:T(4,128)} %intact_ref.1, s32[4,24]{1,0:T(4,128)} %bitcast.9, f32[18,128]{1,0:T(8,128)} %bitcast.8, f32[1]{0:T(128)S(6)} %copy.12.low_ref, f32[1]{0:T(128)S(6)} %copy.13.high_ref), custom_call_target="tpu_custom_call" | custom-call | tf_op jit(solution)/shard_map/filter/pallas_call | solution.py:479
  60.3 1.7 %copy.14 = f32[32,2304]{1,0:T(8,128)} copy(f32[32,2304]{1,0:T(8,128)} %get-tuple-element.4) | data formatting | bytes 589824
  62.0 1.5 %copy.15 = f32[128,128]{1,0:T(8,128)} copy(f32[128,128]{1,0:T(8,128)} %get-tuple-element.5) | data formatting | bytes 131072

commit v3 on v2

--- a/solution.py
+++ b/solution.py
@@ -55,54 +55,80 @@
     return lax.dot_general(left, right, (dims, ((), ())), precision=precision, preferred_element_type=F32)
 
 
-def ritz(col, rows_ref, sums_ref, high_ref, basis_ref, reduced_ref, inv_ref):
-    m = NCOL * COLS
-    groups = m // 8
+def inverse_rows(a):
+    groups = len(a)
+    m = 8 * groups
+    a = list(a)
     lane = lax.broadcasted_iota(jnp.int32, (8, m), 1)
     sub = lax.broadcasted_iota(jnp.int32, (8, m), 0)
-    a = [sums_ref[8 * (g // 4) + g % 4] for g in range(groups)]
-    pivots = []
+
+    def every_row(x, t):
+        return jnp.broadcast_to(x[t:t + 1], (8, m))
+
+    def every_lane(x, k):
+        return jnp.broadcast_to(x[:, k:k + 1], (8, m))
+
+    out = []
     for g in range(groups):
-        c = [[jnp.broadcast_to(a[h][:, 8 * g + t:8 * g + t + 1], (8, m)) for h in range(g, groups)] for t in range(8)]
-        kept = jnp.ones((8, m), F32)
+        z = a[g]
+        c = [every_lane(z, 8 * g + t) for t in range(8)]
+        done = jnp.zeros((8, m), F32)
+        pivots = jnp.ones((8, m), F32)
         for t in range(8):
-            k = 8 * g + t
-            pivot = jnp.broadcast_to(c[t][0][t:t + 1], (8, m))
-            kept = jnp.where(sub == t, pivot, kept)
+            here = sub == t
+            pivot = every_row(c[t], t)
             inv = 1.0 / pivot
-            row = jnp.where(lane == k, 1.0, jnp.broadcast_to(a[g][t:t + 1], (8, m)))
-            facts = [x * inv for x in c[t]]
-            facts[0] = jnp.where(sub > t, facts[0], 0.0)
+            z = jnp.where(lane == 8 * g + t, jnp.where(here, 1.0, 0.0), z)
+            row = every_row(z, t)
+            done = jnp.where(here, row, done)
+            pivots = jnp.where(here, pivot, pivots)
+            row = row * inv
+            fact = jnp.where(here, 0.0, c[t])
+            z = jnp.where(here, row, z) - fact * row
             for u in range(t + 1, 8):
-                same = jnp.broadcast_to(c[t][0][u:u + 1], (8, m))
-                c[u] = [x - f * same for x, f in zip(c[u], facts)]
-            for h in range(g, groups):
-                old = jnp.where((lane == k) & (sub > t) if h == g else lane == k, 0.0, a[h])
-                a[h] = old - facts[h - g] * row
-        pivots.append(kept)
+                same = every_row(c[u], t) * inv
+                c[u] = jnp.where(here, same, c[u]) - fact * same
+        rows = [every_row(z, t) for t in range(8)]
+        panel = (lane >= 8 * g) & (lane < 8 * g + 8)
+        for h in range(g + 1, groups):
+            terms = [every_lane(a[h], 8 * g + t) * rows[t] for t in range(8)]
+            total = ((terms[0] + terms[1]) + (terms[2] + terms[3])) + ((terms[4] + terms[5]) + (terms[6] + terms[7]))
+            a[h] = jnp.where(panel, 0.0, a[h]) - total
+        unit = jnp.where(lane < sub + 8 * g, done, jnp.where(lane == sub + 8 * g, 1.0, 0.0))
+        out.append(unit / jnp.sqrt(pivots))
+    return out
+
+
+def ritz(col, hi_ref, lo_ref, sums_ref, high_ref, basis_ref, reduced_ref, inv_ref):
+    groups = NCOL * COLS // 8
+    rows = inverse_rows([sums_ref[8 * (g // 4) + g % 4] for g in range(groups)])
     for g in range(groups):
-        row = sub + 8 * g
-        unit = jnp.where(lane < row, a[g], jnp.where(lane == row, 1.0, 0.0))
-        inv_ref[8 * g:8 * g + 8, :] = unit / jnp.sqrt(pivots[g])
+        inv_ref[8 * g:8 * g + 8, :] = rows[g]
     mine = inv_ref[pl.ds(col * COLS, COLS), :]
     mine = jnp.concatenate(halves(mine), axis=0)
     for g in range(NBLK // 4):
-        hi, lo = halves(jnp.concatenate([rows_ref[c, g] for c in range(NCOL)], axis=0))
+        hi, lo = (jnp.concatenate([ref[c, g] for c in range(NCOL)], axis=0) for ref in (hi_ref, lo_ref))
         width = hi.shape[1]
         both = contract(mine, hi, ((1,), (0,)))
         low = contract(mine[:COLS], lo, ((1,), (0,)))
         basis_ref[:, width * g:width * (g + 1)] = both[:COLS] + (both[COLS:] + low)
-    inverse = inv_ref[...]
-    proj = jnp.concatenate([sums_ref[8 * (g // 4) + 4 + g % 4] for g in range(groups)], axis=0)
-    half = contract(inverse, proj, ((1,), (0,)), HIGH)
-    reduced_ref[...] = contract(half, inverse, ((1,), (1,)), HIGH) / high_ref[0]
+
+    def three(left, right, dims):
+        both = contract(jnp.concatenate(left, axis=0), right[0], dims)
+        rows = both.shape[0] // 2
+        return both[:rows] + (both[rows:] + contract(left[0], right[1], dims))
+
+    inverse = halves(inv_ref[...])
+    proj = halves(jnp.concatenate([sums_ref[8 * (g // 4) + 4 + g % 4] for g in range(groups)], axis=0))
+    half = halves(three(inverse, proj, ((1,), (0,))))
+    reduced_ref[...] = three(half, inverse, ((1,), (1,))) / high_ref[0]
 
 
 def filter_kernel(
     ntile, zc, block_ref, tiles_ref, intact_ref, adj_ref, diag_ref, low_ref, high_ref,
     basis_ref, reduced_ref,
     tiles_v, intact_v, block_v, diag_in, marks_k, marks_f, marks_in, marks_v, diag_v, merged, qh, qlo, v0, v1, v2, vh, ahead, spill, spill_out, dense, stiff,
-    part, rx1, rx2, sums, inv_v,
+    part, rx1, rx2, sums, inv_v, dense_hi, dense_lo,
     tile_sem, in_sem, ahead_send, ahead_recv, spill_send, spill_recv, x_send, x_recv, r_send, r_recv,
 ):
     tile = lax.axis_index("tile")
@@ -293,10 +319,11 @@
         finish(p, stiffness(vec, p, couple(buf, p)))
         return 0
 
-    def apply(a, buf, vec, finish, hook=None, first=2):
-        lax.fori_loop(first, npair - 2, lambda p, _: inside(buf, vec, finish, p), 0, unroll=2)
-        if hook is not None:
-            hook()
+    def apply(a, buf, vec, finish, runs=((2, 10),), hook=None):
+        for first, last in runs:
+            lax.fori_loop(first, last, lambda p, _: inside(buf, vec, finish, p), 0, unroll=2)
+            if hook is not None:
+                hook(first // 2)
         heads = [couple(buf, p) for p in (0, 1)]
         tails = [couple(buf, npair - 2, 0, 6), couple(buf, npair - 1, 0, 4)]
         ahead_copy(a, vec).wait_recv()
@@ -351,13 +378,27 @@
             return x_copy(ngroup + g, col, g, left)
         return x_copy(2 * ngroup + g, source, g, left)
 
-    def send_groups(rights, lefts):
-        for g in sorted(set(rights + lefts)):
-            for i, x in enumerate(compact(v2, g)):
-                dense[col, g, :, LANES * i:LANES * (i + 1)] = x
-        for a, b in zip(rights, lefts):
-            to_right(a).start()
-            to_left(b).start()
+    def send_group(g):
+        for i, x in enumerate(compact(v2, g)):
+            dense[col, g, :, LANES * i:LANES * (i + 1)] = x
+        to_right(g).start()
+        to_left(g).start()
+
+    def pass_on(g):
+        if g in lower:
+            to_right(g).wait_recv()
+            to_right(g, left).start()
+        else:
+            to_left(g).wait_recv()
+            to_left(g, right).start()
+
+    def pass_on_pair(first):
+        if first == 1:
+            pass_on(2)
+            pass_on(3)
+        else:
+            pass_on(0)
+            pass_on(5)
 
     for n, i in enumerate(order):
         tile_copy(i).wait()
@@ -367,23 +408,17 @@
                 inside(0, v0, finish_first, p - 1)
         if n == 0:
             send_spill(0, 0)
-    apply(0, 0, v0, finish_first, first=npair - chunk - 1)
+    apply(0, 0, v0, finish_first, ((npair - chunk - 1, npair - 2),))
     ahead_copy(1, v1).start()
     send_spill(1, 1)
-    apply(1, 1, v1, finish_filtered, lambda: send_groups((1, 2, 3, 4), (4, 3, 2, 1)))
+    apply(1, 1, v1, finish_filtered, ((2, 4), (8, 10), (4, 6), (6, 8)), send_group)
     ahead_copy(2, v2).start()
     send_spill(2, 0)
-    send_groups((0, 5), (5, 0))
-
-    def pass_on():
-        for a, b in ((1, 4), (2, 3), (0, 5)):
-            to_right(a).wait_recv()
-            to_right(a, left).start()
-            to_left(b).wait_recv()
-            to_left(b, right).start()
-
-    apply(2, 0, v2, finish_stiff)
-    pass_on()
+    send_group(0)
+    send_group(5)
+    pass_on(1)
+    pass_on(4)
+    apply(2, 0, v2, finish_stiff, ((2, 6), (6, 10)), pass_on_pair)
     for g in range(ngroup):
         for i, x in enumerate(compact(v1, g)):
             stiff[g, :, LANES * i:LANES * (i + 1)] = x
@@ -398,6 +433,9 @@
     def against(source, groups):
         lhs = jnp.concatenate([own[g] for g in groups], axis=1)
         parts = [halves(dense[source, g]) for g in groups]
+        for g, (hi, lo) in zip(groups, parts):
+            dense_hi[source, g] = hi
+            dense_lo[source, g] = lo
         rhs = jnp.concatenate([jnp.concatenate([x[i] for x in parts], axis=1) for i in range(2)], axis=0)
         res = contract(lhs, rhs, ((1,), (1,)))
         half = 2 * COLS
@@ -459,7 +497,21 @@
         to_right(g).wait_send()
         to_left(g).wait_send()
         (to_right(g, left) if g in lower else to_left(g, right)).wait_send()
-    ritz(col, dense, sums, high_ref, basis_ref, reduced_ref, inv_v)
+    ritz(col, dense_hi, dense_lo, sums, high_ref, basis_ref, reduced_ref, inv_v)
+
+
+def hand_out_kernel(basis_in, reduced_in, basis_out, reduced_out, basis_v, reduced_v, in_sem, out_sem):
+    parts = [(basis_in.at[pl.ds(8 * i, 8)], basis_v.at[pl.ds(8 * i, 8)], basis_out.at[pl.ds(8 * i, 8)])
+             for i in range(COLS // 8)] + [(reduced_in, reduced_v, reduced_out)]
+    there = [pltpu.make_async_copy(src, mid, in_sem.at[i]) for i, (src, mid, _) in enumerate(parts)]
+    back = [pltpu.make_async_copy(mid, dst, out_sem.at[i]) for i, (_, mid, dst) in enumerate(parts)]
+    for copy in there:
+        copy.start()
+    for first, second in zip(there, back):
+        first.wait()
+        second.start()
+    for copy in back:
+        copy.wait()
 
 
 def local(ntile, block, tiles, intact, adjacency, stiff_diag, cut_low, cut_high):
@@ -476,7 +528,7 @@
     vec = pltpu.VMEM((COLS, NBLK * LANES), F32)
     halo = pltpu.VMEM((3, COLS, REACH * LANES), F32)
     width = 4 * TILE
-    return pl.pallas_call(
+    basis, reduced = pl.pallas_call(
         functools.partial(filter_kernel, ntile, zc),
         out_shape=(
             jax.ShapeDtypeStruct((COLS, NBLK * TILE), F32),
@@ -507,6 +559,8 @@
             pltpu.VMEM((ny, share, LANES), F32),
             pltpu.VMEM((8 * NCOL, share, LANES), F32),
             pltpu.VMEM((NCOL * COLS, NCOL * COLS), F32),
+            pltpu.VMEM((NCOL, NBLK // 4, COLS, width), BF16),
+            pltpu.VMEM((NCOL, NBLK // 4, COLS, width), BF16),
             dma((4,)), dma((3,)), dma((3,)), dma((3,)), dma((3,)), dma((3,)),
             dma((18,)), dma((18,)), dma((3,)), dma((3,)),
         ],
@@ -514,6 +568,23 @@
             collective_id=0, has_side_effects=True, vmem_limit_bytes=57 * 1024 * 1024),
         name="filter",
     )(block, flat, intact, adjacency.T, diag, cut_low, cut_high)
+    return pl.pallas_call(
+        hand_out_kernel,
+        out_shape=(
+            jax.ShapeDtypeStruct((COLS, NBLK * TILE), F32),
+            jax.ShapeDtypeStruct((NCOL * COLS, NCOL * COLS), F32),
+        ),
+        in_specs=[hbm, hbm],
+        out_specs=(hbm, hbm),
+        scratch_shapes=[
+            pltpu.VMEM((COLS, NBLK * TILE), F32),
+            pltpu.VMEM((NCOL * COLS, NCOL * COLS), F32),
+            dma((5,)), dma((5,)),
+        ],
+        compiler_params=pltpu.CompilerParams(vmem_limit_bytes=57 * 1024 * 1024),
+        name="hand_out",
+    )(basis, reduced)
+
 
 def solution(mesh):
     in_specs = (

time: 63.7 us -> 61.1 us (0.959)
  local copies, waits for them, and re-layouts: 3.17 us -> 0 us
    unnamed x2 -> x0, local copies, waits for them, and re-layouts: 3.17 us -> none
    pallas_call x0 -> x1, Pallas kernels: none -> 1.73 us  [local(): pl.pallas_call(hand_out_kernel, out_shape=(jax.ShapeDtypeStruct((COLS, NB...]
    pallas_call x1, Pallas kernels: 58.4 us -> 57.1 us  [local(): pl.pallas_call(functools.partial(filter_kernel, ntile, zc), out_shape=(ja...]
where the time goes in v3:
time: 61.1 us; the launch traced here: 60.9 us
  Pallas kernels  58.8 us (96%)
  between operations  2.09 us (3%)
    pallas_call x1, Pallas kernels, local(): pl.pallas_call(functools.partial(filter_kernel, ntile, zc), out_shape=(ja...  57.1 us
    pallas_call x1, Pallas kernels, local(): pl.pallas_call(hand_out_kernel, out_shape=(jax.ShapeDtypeStruct((COLS, NB...  1.73 us

profile of v3, /device:TPU:1, one launch (start us, length us, event | category | flops | bytes accessed | tf_op | source)
XLA Modules:
  0.0 60.9 jit_solution(6617793548542093173)
XLA Ops:
  1.9 57.1 %filter.1 = (f32[32,2304]{1,0:T(8,128)}, f32[128,128]{1,0:T(8,128)}) custom-call(f32[32,2304]{1,0:T(8,128)} %block_ref.1, f32[6912,128]{1,0:T(8,128)} %bitcast.7, s32[24,4,96]{2,1,0:T(4,128)} %intact_ref.1, s32[4,24]{1,0:T(4,128)} %bitcast.9, f32[18,128]{1,0:T(8,128)} %bitcast.8, f32[1]{0:T(128)S(6)} %copy.10.low_ref, f32[1]{0:T(128)S(6)} %copy.11.high_ref), custom_call_target="tpu_custom_call" | custom-call | tf_op jit(solution)/shard_map/filter/pallas_call | solution.py:531
  59.0 1.7 %hand_out.1 = (f32[32,2304]{1,0:T(8,128)}, f32[128,128]{1,0:T(8,128)}) custom-call(f32[32,2304]{1,0:T(8,128)} %get-tuple-element.4.basis_in, f32[128,128]{1,0:T(8,128)} %get-tuple-element.5.reduced_in), custom_call_target="tpu_custom_call" | custom-call | tf_op jit(solution)/shard_map/hand_out/pallas_call | solution.py:571

commit v4 on v3

--- a/solution.py
+++ b/solution.py
@@ -61,41 +61,30 @@
     a = list(a)
     lane = lax.broadcasted_iota(jnp.int32, (8, m), 1)
     sub = lax.broadcasted_iota(jnp.int32, (8, m), 0)
-
-    def every_row(x, t):
-        return jnp.broadcast_to(x[t:t + 1], (8, m))
-
-    def every_lane(x, k):
-        return jnp.broadcast_to(x[:, k:k + 1], (8, m))
-
+    pivots = []
+    for g in range(groups):
+        c = [[jnp.broadcast_to(a[h][:, 8 * g + t:8 * g + t + 1], (8, m)) for h in range(g, groups)] for t in range(8)]
+        kept = jnp.ones((8, m), F32)
+        for t in range(8):
+            k = 8 * g + t
+            pivot = jnp.broadcast_to(c[t][0][t:t + 1], (8, m))
+            kept = jnp.where(sub == t, pivot, kept)
+            inv = 1.0 / pivot
+            row = jnp.where(lane == k, 1.0, jnp.broadcast_to(a[g][t:t + 1], (8, m)))
+            facts = [x * inv for x in c[t]]
+            facts[0] = jnp.where(sub > t, facts[0], 0.0)
+            for u in range(t + 1, 8):
+                same = jnp.broadcast_to(c[t][0][u:u + 1], (8, m))
+                c[u] = [x - f * same for x, f in zip(c[u], facts)]
+            for h in range(g, groups):
+                old = jnp.where((lane == k) & (sub > t) if h == g else lane == k, 0.0, a[h])
+                a[h] = old - facts[h - g] * row
+        pivots.append(kept)
     out = []
     for g in range(groups):
-        z = a[g]
-        c = [every_lane(z, 8 * g + t) for t in range(8)]
-        done = jnp.zeros((8, m), F32)
-        pivots = jnp.ones((8, m), F32)
-        for t in range(8):
-            here = sub == t
-            pivot = every_row(c[t], t)
-            inv = 1.0 / pivot
-            z = jnp.where(lane == 8 * g + t, jnp.where(here, 1.0, 0.0), z)
-            row = every_row(z, t)
-            done = jnp.where(here, row, done)
-            pivots = jnp.where(here, pivot, pivots)
-            row = row * inv
-            fact = jnp.where(here, 0.0, c[t])
-            z = jnp.where(here, row, z) - fact * row
-            for u in range(t + 1, 8):
-                same = every_row(c[u], t) * inv
-                c[u] = jnp.where(here, same, c[u]) - fact * same
-        rows = [every_row(z, t) for t in range(8)]
-        panel = (lane >= 8 * g) & (lane < 8 * g + 8)
-        for h in range(g + 1, groups):
-            terms = [every_lane(a[h], 8 * g + t) * rows[t] for t in range(8)]
-            total = ((terms[0] + terms[1]) + (terms[2] + terms[3])) + ((terms[4] + terms[5]) + (terms[6] + terms[7]))
-            a[h] = jnp.where(panel, 0.0, a[h]) - total
-        unit = jnp.where(lane < sub + 8 * g, done, jnp.where(lane == sub + 8 * g, 1.0, 0.0))
-        out.append(unit / jnp.sqrt(pivots))
+        row = sub + 8 * g
+        unit = jnp.where(lane < row, a[g], jnp.where(lane == row, 1.0, 0.0))
+        out.append(unit / jnp.sqrt(pivots[g]))
     return out
 
 
@@ -319,13 +308,18 @@
         finish(p, stiffness(vec, p, couple(buf, p)))
         return 0
 
-    def apply(a, buf, vec, finish, runs=((2, 10),), hook=None):
+    def run(buf, vec, finish, first, last):
+        lax.fori_loop(first, last, lambda p, _: inside(buf, vec, finish, p), 0, unroll=2)
+
+    def apply(a, buf, vec, finish, runs, hook=None, between=None):
         for first, last in runs:
-            lax.fori_loop(first, last, lambda p, _: inside(buf, vec, finish, p), 0, unroll=2)
+            run(buf, vec, finish, first, last)
             if hook is not None:
                 hook(first // 2)
         heads = [couple(buf, p) for p in (0, 1)]
         tails = [couple(buf, npair - 2, 0, 6), couple(buf, npair - 1, 0, 4)]
+        if between is not None:
+            between()
         ahead_copy(a, vec).wait_recv()
         keep(buf, npair, jnp.where(has_next, ahead[a], 0.0))
         tails[0] += couple(buf, npair - 2, 6, 8)
@@ -392,11 +386,18 @@
             to_left(g).wait_recv()
             to_left(g, right).start()
 
-    def pass_on_pair(first):
-        if first == 1:
-            pass_on(2)
-            pass_on(3)
-        else:
+    def start_second():
+        for g in (2, 3):
+            run(1, v1, finish_filtered, 2 * g, 2 * g + 2)
+            send_group(g)
+
+    def start_third():
+        run(0, v2, finish_stiff, 4, 8)
+        pass_on(2)
+        pass_on(3)
+
+    def last_relays(g):
+        if g == 4:
             pass_on(0)
             pass_on(5)
 
@@ -408,17 +409,17 @@
                 inside(0, v0, finish_first, p - 1)
         if n == 0:
             send_spill(0, 0)
-    apply(0, 0, v0, finish_first, ((npair - chunk - 1, npair - 2),))
+    apply(0, 0, v0, finish_first, ((npair - chunk - 1, npair - 2),), None, start_second)
     ahead_copy(1, v1).start()
     send_spill(1, 1)
-    apply(1, 1, v1, finish_filtered, ((2, 4), (8, 10), (4, 6), (6, 8)), send_group)
+    apply(1, 1, v1, finish_filtered, ((2, 4), (8, 10)), send_group, start_third)
     ahead_copy(2, v2).start()
     send_spill(2, 0)
     send_group(0)
     send_group(5)
     pass_on(1)
     pass_on(4)
-    apply(2, 0, v2, finish_stiff, ((2, 6), (6, 10)), pass_on_pair)
+    apply(2, 0, v2, finish_stiff, ((2, 4), (8, 10)), last_relays)
     for g in range(ngroup):
         for i, x in enumerate(compact(v1, g)):
             stiff[g, :, LANES * i:LANES * (i + 1)] = x

time: 61.1 us -> 60.9 us (level)
  no operation moved by 1% of the time
where the time goes in v4:
time: 60.9 us; the launch traced here: 60.7 us
  Pallas kernels  58.6 us (96%)
  between operations  2.09 us (3%)
    pallas_call x1, Pallas kernels, local(): pl.pallas_call(functools.partial(filter_kernel, ntile, zc), out_shape=(ja...  56.8 us
    pallas_call x1, Pallas kernels, local(): pl.pallas_call(hand_out_kernel, out_shape=(jax.ShapeDtypeStruct((COLS, NB...  1.73 us

profile of v4, /device:TPU:1, one launch (start us, length us, event | category | flops | bytes accessed | tf_op | source)
XLA Modules:
  0.0 60.7 jit_solution(7904468835463438920)
XLA Ops:
  1.9 56.8 %filter.1 = (f32[32,2304]{1,0:T(8,128)}, f32[128,128]{1,0:T(8,128)}) custom-call(f32[32,2304]{1,0:T(8,128)} %block_ref.1, f32[6912,128]{1,0:T(8,128)} %bitcast.7, s32[24,4,96]{2,1,0:T(4,128)} %intact_ref.1, s32[4,24]{1,0:T(4,128)} %bitcast.9, f32[18,128]{1,0:T(8,128)} %bitcast.8, f32[1]{0:T(128)S(6)} %copy.10.low_ref, f32[1]{0:T(128)S(6)} %copy.11.high_ref), custom_call_target="tpu_custom_call" | custom-call | tf_op jit(solution)/shard_map/filter/pallas_call | solution.py:532
  58.8 1.7 %hand_out.1 = (f32[32,2304]{1,0:T(8,128)}, f32[128,128]{1,0:T(8,128)}) custom-call(f32[32,2304]{1,0:T(8,128)} %get-tuple-element.4.basis_in, f32[128,128]{1,0:T(8,128)} %get-tuple-element.5.reduced_in), custom_call_target="tpu_custom_call" | custom-call | tf_op jit(solution)/shard_map/hand_out/pallas_call | solution.py:572

commit v5 on v4

--- a/solution.py
+++ b/solution.py
@@ -88,7 +88,7 @@
     return out
 
 
-def ritz(col, hi_ref, lo_ref, sums_ref, high_ref, basis_ref, reduced_ref, inv_ref):
+def ritz(col, hi_ref, lo_ref, sums_ref, high_ref, basis_ref, reduced_ref, inv_ref, outs):
     groups = NCOL * COLS // 8
     rows = inverse_rows([sums_ref[8 * (g // 4) + g % 4] for g in range(groups)])
     for g in range(groups):
@@ -102,6 +102,8 @@
         low = contract(mine[:COLS], lo, ((1,), (0,)))
         basis_ref[:, width * g:width * (g + 1)] = both[:COLS] + (both[COLS:] + low)
 
+    outs[0].start()
+
     def three(left, right, dims):
         both = contract(jnp.concatenate(left, axis=0), right[0], dims)
         rows = both.shape[0] // 2
@@ -111,14 +113,15 @@
     proj = halves(jnp.concatenate([sums_ref[8 * (g // 4) + 4 + g % 4] for g in range(groups)], axis=0))
     half = halves(three(inverse, proj, ((1,), (0,))))
     reduced_ref[...] = three(half, inverse, ((1,), (1,))) / high_ref[0]
+    outs[1].start()
 
 
 def filter_kernel(
-    ntile, zc, block_ref, tiles_ref, intact_ref, adj_ref, diag_ref, low_ref, high_ref,
-    basis_ref, reduced_ref,
-    tiles_v, intact_v, block_v, diag_in, marks_k, marks_f, marks_in, marks_v, diag_v, merged, qh, qlo, v0, v1, v2, vh, ahead, spill, spill_out, dense, stiff,
+    ntile, zc, block_ref, tiles_ref, intact_ref, adj_hbm, diag_ref, low_hbm, high_hbm,
+    basis_out, reduced_out,
+    adj_ref, low_ref, high_ref, basis_v, reduced_v, tiles_v, intact_v, block_v, diag_in, marks_k, marks_f, marks_in, marks_v, diag_v, merged, qh, qlo, v0, v1, v2, vh, ahead, spill, spill_out, dense, stiff,
     part, rx1, rx2, sums, inv_v, dense_hi, dense_lo,
-    tile_sem, in_sem, ahead_send, ahead_recv, spill_send, spill_recv, x_send, x_recv, r_send, r_recv,
+    tile_sem, in_sem, out_sem, ahead_send, ahead_recv, spill_send, spill_recv, x_send, x_recv, r_send, r_recv,
 ):
     tile = lax.axis_index("tile")
     col = lax.axis_index("col")
@@ -155,7 +158,8 @@
 
     order = (3, 0, 1, 2)
     small = [pltpu.make_async_copy(src, dst, in_sem.at[i]) for i, (src, dst) in enumerate(
-        ((intact_ref, intact_v), (block_ref, block_v), (diag_ref, diag_in)))]
+        ((intact_ref, intact_v), (block_ref, block_v), (diag_ref, diag_in), (adj_hbm, adj_ref), (low_hbm, low_ref),
+         (high_hbm, high_ref)))]
     for copy in small:
         copy.start()
     for i in order:
@@ -211,7 +215,7 @@
         marks_f[rows, :] = contract(marks_k[rows, 0:16].astype(BF16), pick, ((1,), (0,)))
         return 0
 
-    lax.fori_loop(0, 6, spread_marks, 0, unroll=2)
+    lax.fori_loop(4, 6, spread_marks, 0, unroll=2)
 
     small[1].wait()
     valid32 = lane_id(COLS) < TILE
@@ -224,7 +228,8 @@
             lanes = pl.ds((4 * g + i + REACH) * LANES, LANES)
             vh[0, 0:COLS, lanes] = hi
             vh[0, COLS:2 * COLS, lanes] = lo
-    small[2].wait()
+    for copy in small[2:]:
+        copy.wait()
     xs = [diag_in[pl.ds(i, NBLK // 4, stride=3), :] for i in range(3)]
     for i, piece in enumerate(spread_lanes(*xs)):
         diag_v[pl.ds(i, NBLK // 4, stride=4), :] = piece
@@ -409,6 +414,7 @@
                 inside(0, v0, finish_first, p - 1)
         if n == 0:
             send_spill(0, 0)
+            lax.fori_loop(0, 4, spread_marks, 0, unroll=2)
     apply(0, 0, v0, finish_first, ((npair - chunk - 1, npair - 2),), None, start_second)
     ahead_copy(1, v1).start()
     send_spill(1, 1)
@@ -498,7 +504,11 @@
         to_right(g).wait_send()
         to_left(g).wait_send()
         (to_right(g, left) if g in lower else to_left(g, right)).wait_send()
-    ritz(col, dense_hi, dense_lo, sums, high_ref, basis_ref, reduced_ref, inv_v)
+    outs = [pltpu.make_async_copy(src, dst, out_sem.at[i]) for i, (src, dst) in enumerate(
+        ((basis_v, basis_out), (reduced_v, reduced_out)))]
+    ritz(col, dense_hi, dense_lo, sums, high_ref, basis_v, reduced_v, inv_v, outs)
+    for copy in outs:
+        copy.wait()
 
 
 def hand_out_kernel(basis_in, reduced_in, basis_out, reduced_out, basis_v, reduced_v, in_sem, out_sem):
@@ -521,8 +531,6 @@
     share = 2 * COLS // 8
     flat = tiles.reshape(NBLK, 4, 72, LANES).transpose(0, 2, 1, 3).reshape(NBLK * 4 * 72, LANES)
     diag = stiff_diag.reshape(NBLK * TILE // LANES, LANES)
-    vm = pl.BlockSpec(memory_space=pltpu.VMEM)
-    sm = pl.BlockSpec(memory_space=pltpu.SMEM)
     hbm = pl.BlockSpec(memory_space=pltpu.HBM)
     npair = NBLK // 2
     dma = pltpu.SemaphoreType.DMA
@@ -535,9 +543,14 @@
             jax.ShapeDtypeStruct((COLS, NBLK * TILE), F32),
             jax.ShapeDtypeStruct((NCOL * COLS, NCOL * COLS), F32),
         ),
-        in_specs=[hbm, hbm, hbm, sm, hbm, sm, sm],
-        out_specs=(vm, vm),
+        in_specs=[hbm] * 7,
+        out_specs=(hbm, hbm),
         scratch_shapes=[
+            pltpu.SMEM((4, NBLK), jnp.int32),
+            pltpu.SMEM((1,), F32),
+            pltpu.SMEM((1,), F32),
+            pltpu.VMEM((COLS, NBLK * TILE), F32),
+            pltpu.VMEM((NCOL * COLS, NCOL * COLS), F32),
             pltpu.VMEM((NBLK * 4 * 72, LANES), F32),
             pltpu.VMEM((NBLK, 4, TILE), jnp.int32),
             pltpu.VMEM((COLS, NBLK * TILE), F32),
@@ -562,7 +575,7 @@
             pltpu.VMEM((NCOL * COLS, NCOL * COLS), F32),
             pltpu.VMEM((NCOL, NBLK // 4, COLS, width), BF16),
             pltpu.VMEM((NCOL, NBLK // 4, COLS, width), BF16),
-            dma((4,)), dma((3,)), dma((3,)), dma((3,)), dma((3,)), dma((3,)),
+            dma((4,)), dma((6,)), dma((2,)), dma((3,)), dma((3,)), dma((3,)), dma((3,)),
             dma((18,)), dma((18,)), dma((3,)), dma((3,)),
         ],
         compiler_params=pltpu.CompilerParams(

time: 60.9 us -> 60.9 us (level)
  no operation moved by 1% of the time
where the time goes in v5:
time: 60.9 us; the launch traced here: 60.7 us
  Pallas kernels  58.6 us (96%)
  between operations  2.09 us (3%)
    pallas_call x1, Pallas kernels, local(): pl.pallas_call(functools.partial(filter_kernel, ntile, zc), out_shape=(ja...  56.9 us
    pallas_call x1, Pallas kernels, local(): pl.pallas_call(hand_out_kernel, out_shape=(jax.ShapeDtypeStruct((COLS, NB...  1.73 us

profile of v5, /device:TPU:1, one launch (start us, length us, event | category | flops | bytes accessed | tf_op | source)
XLA Modules:
  0.0 60.7 jit_solution(17519650035274374833)
XLA Ops:
  1.9 56.9 %filter.1 = (f32[32,2304]{1,0:T(8,128)}, f32[128,128]{1,0:T(8,128)}) custom-call(f32[32,2304]{1,0:T(8,128)} %block_ref.1, f32[6912,128]{1,0:T(8,128)} %bitcast.7, s32[24,4,96]{2,1,0:T(4,128)} %intact_ref.1, s32[4,24]{1,0:T(4,128)} %bitcast.9, f32[18,128]{1,0:T(8,128)} %bitcast.8, f32[1]{0:T(128)S(6)} %copy.10.low_hbm, f32[1]{0:T(128)S(6)} %copy.11.high_hbm), custom_call_target="tpu_custom_call" | custom-call | tf_op jit(solution)/shard_map/filter/pallas_call | solution.py:540
  58.8 1.7 %hand_out.1 = (f32[32,2304]{1,0:T(8,128)}, f32[128,128]{1,0:T(8,128)}) custom-call(f32[32,2304]{1,0:T(8,128)} %get-tuple-element.4.basis_in, f32[128,128]{1,0:T(8,128)} %get-tuple-element.5.reduced_in), custom_call_target="tpu_custom_call" | custom-call | tf_op jit(solution)/shard_map/hand_out/pallas_call | solution.py:585

commit v6 on v5

--- a/solution.py
+++ b/solution.py
@@ -316,7 +316,7 @@
     def run(buf, vec, finish, first, last):
         lax.fori_loop(first, last, lambda p, _: inside(buf, vec, finish, p), 0, unroll=2)
 
-    def apply(a, buf, vec, finish, runs, hook=None, between=None):
+    def apply(a, buf, vec, finish, runs, hook=None, between=None, after_tails=None):
         for first, last in runs:
             run(buf, vec, finish, first, last)
             if hook is not None:
@@ -331,6 +331,8 @@
         tails[1] += couple(buf, npair - 1, 4, 8)
         for i in range(2):
             finish(npair - 2 + i, stiffness(vec, npair - 2 + i, tails[i]))
+        if after_tails is not None:
+            after_tails()
         spill_copy(a).wait_recv()
         extra = jnp.where(has_prev, spill[a], 0.0)
         heads[0] += extra[:, 0:2 * LANES]
@@ -377,9 +379,12 @@
             return x_copy(ngroup + g, col, g, left)
         return x_copy(2 * ngroup + g, source, g, left)
 
-    def send_group(g):
+    def pack_group(g):
         for i, x in enumerate(compact(v2, g)):
             dense[col, g, :, LANES * i:LANES * (i + 1)] = x
+
+    def send_group(g):
+        pack_group(g)
         to_right(g).start()
         to_left(g).start()
 
@@ -415,14 +420,17 @@
         if n == 0:
             send_spill(0, 0)
             lax.fori_loop(0, 4, spread_marks, 0, unroll=2)
-    apply(0, 0, v0, finish_first, ((npair - chunk - 1, npair - 2),), None, start_second)
+    apply(0, 0, v0, finish_first, ((npair - chunk - 1, npair - 2),), None, start_second,
+          lambda: send_spill(1, 1))
     ahead_copy(1, v1).start()
-    send_spill(1, 1)
-    apply(1, 1, v1, finish_filtered, ((2, 4), (8, 10)), send_group, start_third)
+    apply(1, 1, v1, finish_filtered, ((2, 4), (8, 10)), send_group, start_third, lambda: send_spill(2, 0))
     ahead_copy(2, v2).start()
-    send_spill(2, 0)
-    send_group(0)
-    send_group(5)
+    pack_group(0)
+    to_right(0).start()
+    pack_group(5)
+    to_left(5).start()
+    to_right(5).start()
+    to_left(0).start()
     pass_on(1)
     pass_on(4)
     apply(2, 0, v2, finish_stiff, ((2, 4), (8, 10)), last_relays)

time: 60.9 us -> 59.8 us (0.982)
  Pallas kernels: 58.6 us -> 57.5 us
    pallas_call x1, Pallas kernels: 56.9 us -> 55.8 us  [local(): pl.pallas_call(functools.partial(filter_kernel, ntile, zc), out_shape=(ja...]
where the time goes in v6:
time: 59.8 us; the launch traced here: 59.6 us
  Pallas kernels  57.5 us (96%)
  between operations  2.09 us (3%)
    pallas_call x1, Pallas kernels, local(): pl.pallas_call(functools.partial(filter_kernel, ntile, zc), out_shape=(ja...  55.8 us
    pallas_call x1, Pallas kernels, local(): pl.pallas_call(hand_out_kernel, out_shape=(jax.ShapeDtypeStruct((COLS, NB...  1.73 us

profile of v6, /device:TPU:1, one launch (start us, length us, event | category | flops | bytes accessed | tf_op | source)
XLA Modules:
  0.0 59.6 jit_solution(16793618611199588867)
XLA Ops:
  1.9 55.8 %filter.1 = (f32[32,2304]{1,0:T(8,128)}, f32[128,128]{1,0:T(8,128)}) custom-call(f32[32,2304]{1,0:T(8,128)} %block_ref.1, f32[6912,128]{1,0:T(8,128)} %bitcast.7, s32[24,4,96]{2,1,0:T(4,128)} %intact_ref.1, s32[4,24]{1,0:T(4,128)} %bitcast.9, f32[18,128]{1,0:T(8,128)} %bitcast.8, f32[1]{0:T(128)S(6)} %copy.10.low_hbm, f32[1]{0:T(128)S(6)} %copy.11.high_hbm), custom_call_target="tpu_custom_call" | custom-call | tf_op jit(solution)/shard_map/filter/pallas_call | solution.py:548
  57.7 1.7 %hand_out.1 = (f32[32,2304]{1,0:T(8,128)}, f32[128,128]{1,0:T(8,128)}) custom-call(f32[32,2304]{1,0:T(8,128)} %get-tuple-element.4.basis_in, f32[128,128]{1,0:T(8,128)} %get-tuple-element.5.reduced_in), custom_call_target="tpu_custom_call" | custom-call | tf_op jit(solution)/shard_map/hand_out/pallas_call | solution.py:593

commit v7 on v6

--- a/solution.py
+++ b/solution.py
@@ -316,7 +316,8 @@
     def run(buf, vec, finish, first, last):
         lax.fori_loop(first, last, lambda p, _: inside(buf, vec, finish, p), 0, unroll=2)
 
-    def apply(a, buf, vec, finish, runs, hook=None, between=None, after_tails=None):
+    def apply(a, buf, vec, finish, runs, hook=None, between=None, after_tails=None,
+              after_heads=None):
         for first, last in runs:
             run(buf, vec, finish, first, last)
             if hook is not None:
@@ -325,20 +326,31 @@
         tails = [couple(buf, npair - 2, 0, 6), couple(buf, npair - 1, 0, 4)]
         if between is not None:
             between()
-        ahead_copy(a, vec).wait_recv()
-        keep(buf, npair, jnp.where(has_next, ahead[a], 0.0))
-        tails[0] += couple(buf, npair - 2, 6, 8)
-        tails[1] += couple(buf, npair - 1, 4, 8)
-        for i in range(2):
-            finish(npair - 2 + i, stiffness(vec, npair - 2 + i, tails[i]))
-        if after_tails is not None:
-            after_tails()
-        spill_copy(a).wait_recv()
-        extra = jnp.where(has_prev, spill[a], 0.0)
-        heads[0] += extra[:, 0:2 * LANES]
-        heads[1] += jnp.concatenate([extra[:, 2 * LANES:], jnp.zeros((COLS, LANES), F32)], axis=1)
-        for i in range(2):
-            finish(i, stiffness(vec, i, heads[i]))
+
+        def end_tails():
+            ahead_copy(a, vec).wait_recv()
+            keep(buf, npair, jnp.where(has_next, ahead[a], 0.0))
+            late = [couple(buf, npair - 2, 6, 8), couple(buf, npair - 1, 4, 8)]
+            for i in range(2):
+                finish(npair - 2 + i, stiffness(vec, npair - 2 + i, tails[i] + late[i]))
+            if after_tails is not None:
+                after_tails()
+
+        def end_heads():
+            spill_copy(a).wait_recv()
+            extra = jnp.where(has_prev, spill[a], 0.0)
+            finish(0, stiffness(vec, 0, heads[0] + extra[:, 0:2 * LANES]))
+            rest = jnp.concatenate([extra[:, 2 * LANES:], jnp.zeros((COLS, LANES), F32)], axis=1)
+            finish(1, stiffness(vec, 1, heads[1] + rest))
+            if after_heads is not None:
+                after_heads()
+
+        if a == 1:
+            end_heads()
+            end_tails()
+        else:
+            end_tails()
+            end_heads()
         ahead_copy(a, vec).wait_send()
         spill_copy(a).wait_send()
 
@@ -421,16 +433,19 @@
             send_spill(0, 0)
             lax.fori_loop(0, 4, spread_marks, 0, unroll=2)
     apply(0, 0, v0, finish_first, ((npair - chunk - 1, npair - 2),), None, start_second,
-          lambda: send_spill(1, 1))
-    ahead_copy(1, v1).start()
-    apply(1, 1, v1, finish_filtered, ((2, 4), (8, 10)), send_group, start_third, lambda: send_spill(2, 0))
-    ahead_copy(2, v2).start()
-    pack_group(0)
-    to_right(0).start()
-    pack_group(5)
-    to_left(5).start()
-    to_right(5).start()
-    to_left(0).start()
+          lambda: send_spill(1, 1), lambda: ahead_copy(1, v1).start())
+
+    def after_second_tails():
+        pack_group(5)
+        to_left(5).start()
+        to_right(5).start()
+        send_spill(2, 0)
+
+    def after_second_heads():
+        send_group(0)
+        ahead_copy(2, v2).start()
+
+    apply(1, 1, v1, finish_filtered, ((2, 4), (8, 10)), send_group, start_third, after_second_tails, after_second_heads)
     pass_on(1)
     pass_on(4)
     apply(2, 0, v2, finish_stiff, ((2, 4), (8, 10)), last_relays)

time: 59.8 us -> 61 us (1.020)
  Pallas kernels: 57.5 us -> 58.7 us
    pallas_call x1, Pallas kernels: 55.8 us -> 57 us  [local(): pl.pallas_call(functools.partial(filter_kernel, ntile, zc), out_shape=(ja...]
where the time goes in v7:
time: 61 us; the launch traced here: 60.8 us
  Pallas kernels  58.7 us (96%)
  between operations  2.09 us (3%)
    pallas_call x1, Pallas kernels, local(): pl.pallas_call(functools.partial(filter_kernel, ntile, zc), out_shape=(ja...  57 us
    pallas_call x1, Pallas kernels, local(): pl.pallas_call(hand_out_kernel, out_shape=(jax.ShapeDtypeStruct((COLS, NB...  1.73 us

profile of v7, /device:TPU:1, one launch (start us, length us, event | category | flops | bytes accessed | tf_op | source)
XLA Modules:
  0.0 60.8 jit_solution(180866483683074694)
XLA Ops:
  1.9 57.0 %filter.1 = (f32[32,2304]{1,0:T(8,128)}, f32[128,128]{1,0:T(8,128)}) custom-call(f32[32,2304]{1,0:T(8,128)} %block_ref.1, f32[6912,128]{1,0:T(8,128)} %bitcast.7, s32[24,4,96]{2,1,0:T(4,128)} %intact_ref.1, s32[4,24]{1,0:T(4,128)} %bitcast.9, f32[18,128]{1,0:T(8,128)} %bitcast.8, f32[1]{0:T(128)S(6)} %copy.10.low_hbm, f32[1]{0:T(128)S(6)} %copy.11.high_hbm), custom_call_target="tpu_custom_call" | custom-call | tf_op jit(solution)/shard_map/filter/pallas_call | solution.py:563
  58.9 1.7 %hand_out.1 = (f32[32,2304]{1,0:T(8,128)}, f32[128,128]{1,0:T(8,128)}) custom-call(f32[32,2304]{1,0:T(8,128)} %get-tuple-element.4.basis_in, f32[128,128]{1,0:T(8,128)} %get-tuple-element.5.reduced_in), custom_call_target="tpu_custom_call" | custom-call | tf_op jit(solution)/shard_map/hand_out/pallas_call | solution.py:608
